TPU v7x, 128 devices: a whole 4x4x4 slice. The times are simulated.
128 devices in a mesh: face: 4 (over x_hi, core), tile: 32 (over x_lo, z, y).
Axes of the slice: x: 4 (x_hi: 2, x_lo: 2; x = x_hi * 2 + x_lo), y: 4, z: 4, core: 2. Of those that a mesh axis runs over, the one named last changes fastest.
Arguments:
- atmos: bfloat16 [64, 768, 2048], P(None, 'tile', 'face'), may hold values from -6 to 6
- ocean: bfloat16 [64, 262144], P(None, ('face', 'tile')), may hold values from -6 to 6
- surface_heat_weight: float32 [64], replicated, may hold values from -4 to 4
- air_conv_first_weight: bfloat16 [3, 3, 64, 64], replicated, may hold values from -0.25 to 0.25
- air_conv_second_weight: bfloat16 [3, 3, 64, 64], replicated, may hold values from -0.25 to 0.25
- marine_conv_first_weight: bfloat16 [9, 64, 64], replicated, may hold values from -0.25 to 0.25
- marine_conv_second_weight: bfloat16 [9, 64, 64], replicated, may hold values from -0.25 to 0.25
- marine_coupling_slot: int32 [262144], P(('face', 'tile')), may hold values from 0 to 4095, as said below
- coupling_air_cells: int32 [128, 4096], P(('face', 'tile')), may hold values from 0 to 12287
- marine_neighbour_index: int32 [9, 262144], P(None, ('face', 'tile')), may hold values from 0 to 2559, as said below
Outputs:
- atmos_next: bfloat16 [64, 768, 2048], P(None, 'tile', 'face')
- ocean_next: bfloat16 [64, 262144], P(None, ('face', 'tile'))
Inputs may be any that keep to these rules, and one draw needn't show every extreme that they name: `marine_coupling_slot`: within one ocean device's 2048 entries the values are distinct; value // 32 is the atmosphere device serving the cell, so no atmosphere device serves more than 32 cells of one ocean device, and on every ocean device some atmosphere device serves exactly 32. `marine_neighbour_index`: entry [k, g] lies within 256 of the cell's own position 256 + g % 2048; every device's entries reach both ends.
All inputs are finite; a program needn't handle non-finite values.
Results may differ from a plain program's by a relative error of at most 0.0064.
Values may be sent and summed in bfloat16 or wider, within the bound.
A program may use at most 128 MiB of HBM per device.

v0:
```python
import jax
import jax.numpy as jnp
from jax import lax
from jax.experimental import pallas as pl
from jax.experimental.pallas import tpu as pltpu
from jax.sharding import PartitionSpec as P

MESH = pl.DeviceIdType.MESH
BF = jnp.bfloat16
F32 = jnp.float32
I32 = jnp.int32
FACES = 4
TILES = 32
DEVICES = 128
CAP = 32
CH = 64
AR = 24
AC = 512
OCN = 2048
SLOTS = 4096
HALO = 256
EXT = OCN + 2 * HALO
RING = AC + 128
TAPS = 9


def iota(shape, dim):
    return lax.broadcasted_iota(I32, shape, dim)


def dot(a, b):
    return jnp.dot(a, b, preferred_element_type=F32)


def dot_nt(a, b):
    return lax.dot_general(a, b, (((1,), (1,)), ((), ())), preferred_element_type=F32)


def onehot(mask):
    return jnp.where(mask, 1.0, 0.0).astype(BF)


def where_of(number):
    return (lax.div(number, TILES), lax.rem(number, TILES))


def kernel(
    air, ocean, heat, w1, w2, m1, m2, slot, cells, taps,
    air_out, ocean_out,
    vsend, vrecv, cols, rcols, rrows, sst, sx, hx, acc, weights, picked_cols, table, onecol,
    gsend, grecv, arrived, oneslot, mweights, window, hwindow, picked,
    a_send, a_recv, r_send, r_recv, s_send, s_recv, g_send, g_recv, o_send, o_recv,
):
    face = lax.axis_index("face")
    tile = lax.axis_index("tile")
    me = face * TILES + tile

    barrier = pltpu.get_barrier_semaphore()

    def greet(step, carry):
        other = lax.rem(me + step, DEVICES)
        pl.semaphore_signal(barrier, inc=1, device_id=where_of(other), device_id_type=MESH)
        return carry

    lax.fori_loop(1, DEVICES, greet, 0)

    slots = slot[...]
    heat_row = ocean[0:16, :].astype(F32)[0:1]
    source = onehot(iota((DEVICES, OCN), 0) == slots // CAP)
    place = iota((DEVICES, OCN), 0)
    position = slots % CAP
    values = jnp.where(place == position, heat_row, 0.0)
    values = jnp.where(place == position + CAP, 1.0, values).astype(BF)
    vsend[:, 0, :] = dot_nt(source, values)

    lane = iota((CH, 128), 1)

    def pack_row(row, carry):
        left, right = carry
        first = jnp.where(lane < 2, air[row, :, 0:128].astype(F32), 0.0)
        last = jnp.where(lane >= 126, air[row, :, AC - 128 : AC].astype(F32), 0.0)
        left = left + pltpu.roll(first, 2 * row, 1)
        right = right + pltpu.roll(last, 2 * row + 2, 1)
        return left, right

    zero = jnp.zeros((CH, 128), F32)
    left, right = lax.fori_loop(0, AR, pack_row, (zero, zero))
    cols[0] = left.astype(BF)
    cols[1] = right.astype(BF)

    pl.semaphore_wait(barrier, DEVICES - 1)

    def send_values(step, carry):
        other = lax.rem(me + step, DEVICES)
        pltpu.make_async_remote_copy(
            src_ref=vsend.at[other], dst_ref=vrecv.at[me], send_sem=a_send, recv_sem=a_recv,
            device_id=where_of(other), device_id_type=MESH,
        ).start()
        return carry

    lax.fori_loop(1, DEVICES, send_values, 0)
    vrecv[me] = vsend[me]

    up = lax.rem(tile + TILES - 1, TILES)
    down = lax.rem(tile + 1, TILES)
    west = lax.rem(face + FACES - 1, FACES)
    east = lax.rem(face + 1, FACES)
    around = (
        (face, up), (face, down), (west, tile), (east, tile),
        (west, up), (west, down), (east, up), (east, down),
    )

    def rim(number, src, dst, send, recv):
        return pltpu.make_async_remote_copy(
            src_ref=src, dst_ref=dst, send_sem=send.at[number], recv_sem=recv.at[number],
            device_id=around[number], device_id_type=MESH,
        )

    air_rims = [
        rim(0, air.at[0:2], rrows.at[1], r_send, r_recv),
        rim(1, air.at[AR - 2 : AR], rrows.at[0], r_send, r_recv),
        rim(2, cols.at[0], rcols.at[1], r_send, r_recv),
        rim(3, cols.at[1], rcols.at[0], r_send, r_recv),
        rim(4, cols.at[0], rcols.at[5], r_send, r_recv),
        rim(5, cols.at[0], rcols.at[3], r_send, r_recv),
        rim(6, cols.at[1], rcols.at[4], r_send, r_recv),
        rim(7, cols.at[1], rcols.at[2], r_send, r_recv),
    ]
    for copy in air_rims:
        copy.start()

    def make_columns(step, carry):
        base = pl.multiple_of(step * 256, 256)
        column = cells[0:1, pl.ds(base, 256)] % AC
        onecol[:, pl.ds(base, 256)] = onehot(iota((AC, 256), 0) == column)
        return carry

    lax.fori_loop(0, SLOTS // 256, make_columns, 0)
    for number, weight in enumerate((w1, w2)):
        for row_tap in range(3):
            for col_tap in range(3):
                weights[number, row_tap * CH : (row_tap + 1) * CH, col_tap * CH : (col_tap + 1) * CH] = weight[
                    row_tap, col_tap
                ]
    for number, weight in enumerate((m1, m2)):
        for tap in range(TAPS):
            mweights[number, :, tap * CH : (tap + 1) * CH] = weight[tap]
    channel_weight = jnp.sum(
        jnp.where(iota((CH, CH), 0) == iota((CH, CH), 1), heat[...], 0.0), axis=1, keepdims=True
    )

    for copy in air_rims:
        copy.wait()

    def ring_block(row, left, right):
        from_right = pltpu.roll(right, lax.rem(128 - 2 * row, 128), 1)
        from_left = pltpu.roll(left, lax.rem(254 - 2 * row, 128), 1)
        return jnp.where(lane < 64, from_right, from_left).astype(BF)

    def extend(row, carry):
        sx[row + 2, :, 0:AC] = air[row]
        sx[row + 2, :, AC:RING] = ring_block(row, rcols[0].astype(F32), rcols[1].astype(F32))
        return carry

    lax.fori_loop(0, AR, extend, 0)
    for row in range(2):
        sx[row, :, 0:AC] = rrows[0, row]
        sx[row, :, AC:RING] = ring_block(jnp.int32(AR - 2 + row), rcols[2].astype(F32), rcols[3].astype(F32))
        sx[AR + 2 + row, :, 0:AC] = rrows[1, row]
        sx[AR + 2 + row, :, AC:RING] = ring_block(jnp.int32(row), rcols[4].astype(F32), rcols[5].astype(F32))

    pltpu.make_async_copy(vrecv.at[pl.ds(0, DEVICES - 1)], vrecv.at[pl.ds(0, DEVICES - 1)], a_recv).wait()
    got = vrecv[:, 0, :].astype(BF)
    square = (DEVICES, 128)
    mine = iota(square, 0) % 4 == iota(square, 1) // CAP
    group = onehot(iota((CAP, DEVICES), 0) == iota((CAP, DEVICES), 1) // 4)
    for kind in range(2):
        expand = onehot(iota(square, 0) - CAP * kind == iota(square, 1) % CAP)
        spread = jnp.where(mine, dot(got, expand), 0.0).astype(BF)
        table[kind] = dot(group, spread)

    def make_rows(step, carry):
        base = pl.multiple_of(step * 128, 128)
        row = cells[0:1, pl.ds(base, 128)] // AC
        hit = iota((CAP, 128), 0) == row
        for kind in range(2):
            picked_cols[CAP * kind : CAP * (kind + 1), pl.ds(base, 128)] = jnp.where(
                hit, table[kind, pl.ds(step, 1), :], 0.0
            ).astype(BF)
        return carry

    lax.fori_loop(0, SLOTS // 128, make_rows, 0)
    sums = dot_nt(picked_cols[...], onecol[...])
    sst[8 : 8 + AR, 128 : 128 + AC] = sums[0:AR] / jnp.maximum(sums[CAP : CAP + AR], 1.0)

    top, low, far = 128, 640, 768
    sst_rims = [
        rim(0, sst.at[8:16, top:low], sst.at[32:40, top:low], s_send, s_recv),
        rim(1, sst.at[24:32, top:low], sst.at[0:8, top:low], s_send, s_recv),
        rim(2, sst.at[8:32, 128:256], sst.at[8:32, low:far], s_send, s_recv),
        rim(3, sst.at[8:32, 512:640], sst.at[8:32, 0:128], s_send, s_recv),
        rim(4, sst.at[8:16, 128:256], sst.at[32:40, low:far], s_send, s_recv),
        rim(5, sst.at[24:32, 128:256], sst.at[0:8, low:far], s_send, s_recv),
        rim(6, sst.at[8:16, 512:640], sst.at[32:40, 0:128], s_send, s_recv),
        rim(7, sst.at[24:32, 512:640], sst.at[0:8, 0:128], s_send, s_recv),
    ]
    for copy in sst_rims:
        copy.start()
    for copy in sst_rims:
        copy.wait()

    low_lane = iota((1, 128), 1) < 64

    def begin(row, carry):
        line = sst[pl.ds(row + 6, 1), :]
        ring = jnp.concatenate(
            [line[:, 128 : 128 + AC], jnp.where(low_lane, line[:, 640:768], line[:, 0:128])], axis=1
        )
        state = sx[row].astype(F32) + channel_weight * ring
        inside = jnp.logical_and(jnp.logical_or(row >= 2, tile > 0), jnp.logical_or(row < AR + 2, tile < TILES - 1))
        sx[row] = jnp.where(inside, state, 0.0).astype(BF)
        return carry

    lax.fori_loop(0, AR + 4, begin, 0)

    def three(x, width):
        wide = x.astype(F32)
        before = pltpu.roll(wide, 1, 1).astype(BF)[:, 0:width]
        after = pltpu.roll(wide, RING - 1, 1).astype(BF)[:, 0:width]
        return jnp.concatenate([before, x[:, 0:width], after], axis=0)

    def first_conv(row, carry):
        part = dot(weights[0], three(sx[row], RING))
        total = acc[0] + part[2 * CH : 3 * CH]
        acc[0] = acc[1] + part[CH : 2 * CH]
        acc[1] = part[0:CH]
        middle = row - 2
        inside = jnp.logical_and(jnp.logical_or(middle >= 1, tile > 0), jnp.logical_or(middle < AR + 1, tile < TILES - 1))
        hidden = jnp.where(inside, jax.nn.gelu(total, approximate=True), 0.0)
        hx[jnp.maximum(middle, 0)] = hidden.astype(BF)
        return carry

    lax.fori_loop(0, AR + 4, first_conv, 0)

    def second_conv(row, carry):
        part = dot(weights[1], three(hx[row], AC))
        total = acc[0, :, 0:AC] + part[2 * CH : 3 * CH]
        acc[0, :, 0:AC] = acc[1, :, 0:AC] + part[CH : 2 * CH]
        acc[1, :, 0:AC] = part[0:CH]
        middle = jnp.maximum(row - 2, 0)
        air_out[middle] = (sx[middle + 2, :, 0:AC].astype(F32) + total).astype(BF)
        return carry

    lax.fori_loop(0, AR + 2, second_conv, 0)

    def coupling(step, carry):
        block = lax.rem(lax.div(me, 8) + step, DEVICES // 8)
        base = pl.multiple_of(block * 256, 256)
        row = cells[0:1, pl.ds(base, 256)] // AC
        select = onecol[:, pl.ds(base, 256)]
        state = jnp.zeros((CH, 256), F32)
        for part in range(AR // 4):
            rows = air_out[part * 4 : part * 4 + 4].reshape(4 * CH, AC)
            found = dot(rows, select)
            for inner in range(4):
                state = jnp.where(row == part * 4 + inner, found[inner * CH : (inner + 1) * CH], state)
        flat = jnp.transpose(state).reshape(8, CAP, CH)
        pair = jnp.concatenate([flat[:, 0:16], flat[:, 16:32]], axis=2)
        gsend[pl.ds(pl.multiple_of(block * 8, 8), 8)] = pair.astype(BF)
        for inner in range(8):
            other = block * 8 + inner

            @pl.when(other != me)
            def _():
                pltpu.make_async_remote_copy(
                    src_ref=gsend.at[other], dst_ref=grecv.at[me], send_sem=g_send, recv_sem=g_recv,
                    device_id=where_of(other), device_id_type=MESH,
                ).start()

        return carry

    lax.fori_loop(0, DEVICES // 8, coupling, 0)
    grecv[me] = gsend[me]

    def make_slots(step, carry):
        base = pl.multiple_of(step * 256, 256)
        mark = slot[0:1, pl.ds(base, 256)]
        row = mark // CAP * 16 + mark % 16

        def fill(part, inner_carry):
            first = pl.multiple_of(part * 256, 256)
            oneslot[pl.ds(first, 256), pl.ds(base, 256)] = onehot(iota((256, 256), 0) + first == row)
            return inner_carry

        return lax.fori_loop(0, OCN // 256, fill, carry)

    lax.fori_loop(0, OCN // 256, make_slots, 0)
    pltpu.make_async_copy(grecv.at[pl.ds(0, DEVICES - 1)], grecv.at[pl.ds(0, DEVICES - 1)], g_recv).wait()

    def turn(step, carry):
        eight = grecv[pl.ds(pl.multiple_of(step * 8, 8), 8)].reshape(128, 128)
        arrived[:, pl.ds(pl.multiple_of(step * 128, 128), 128)] = jnp.transpose(eight.astype(F32)).astype(BF)
        return carry

    lax.fori_loop(0, DEVICES // 8, turn, 0)

    def force(step, carry):
        base = pl.multiple_of(step * 256, 256)
        late = (slot[0:1, pl.ds(base, 256)] // 16) % 2 == 1
        found = dot(arrived[...], oneslot[:, pl.ds(base, 256)])
        forcing = jnp.where(late, found[CH : 2 * CH], found[0:CH])
        begun = ocean[:, pl.ds(base, 256)].astype(F32) + forcing
        window[:, pl.ds(base + HALO, 256)] = begun.astype(BF).astype(F32)
        return carry

    lax.fori_loop(0, OCN // 256, force, 0)

    before = where_of(lax.rem(me + DEVICES - 1, DEVICES))
    after = where_of(lax.rem(me + 1, DEVICES))

    def ocean_rims(buffer, first):
        return [
            pltpu.make_async_remote_copy(
                src_ref=buffer.at[:, HALO : 2 * HALO], dst_ref=buffer.at[:, EXT - HALO : EXT],
                send_sem=o_send.at[first], recv_sem=o_recv.at[first], device_id=before, device_id_type=MESH,
            ),
            pltpu.make_async_remote_copy(
                src_ref=buffer.at[:, OCN : OCN + HALO], dst_ref=buffer.at[:, 0:HALO],
                send_sem=o_send.at[first + 1], recv_sem=o_recv.at[first + 1], device_id=after, device_id_type=MESH,
            ),
        ]

    def mix(buffer, number, block):
        for half in range(2):
            base = pl.multiple_of(block * 256 + half * 128, 128)
            parts = [
                [
                    buffer[group * 8 : (group + 1) * 8, pl.ds(pl.multiple_of(base + part * 128, 128), 128)]
                    for part in range(5)
                ]
                for group in range(CH // 8)
            ]
            for tap in range(TAPS):
                index = jnp.broadcast_to(taps[tap : tap + 1, pl.ds(base, 128)] - base, (8, 128))
                inner = index % 128
                part_of = index // 128
                groups = []
                for group in range(CH // 8):
                    found = jnp.take_along_axis(parts[group][0], inner, axis=1)
                    for part in range(1, 5):
                        found = jnp.where(
                            part_of == part, jnp.take_along_axis(parts[group][part], inner, axis=1), found
                        )
                    groups.append(found)
                picked[tap * CH : (tap + 1) * CH, half * 128 : (half + 1) * 128] = jnp.concatenate(
                    groups, axis=0
                ).astype(BF)
        return dot(mweights[number], picked[...])

    def hidden_block(block):
        total = mix(window, 0, block)
        base = pl.multiple_of(block * 256, 256)
        hwindow[:, pl.ds(base + HALO, 256)] = jax.nn.gelu(total, approximate=True).astype(BF).astype(F32)

    def last_block(block):
        total = mix(hwindow, 1, block)
        base = pl.multiple_of(block * 256, 256)
        ocean_out[:, pl.ds(base, 256)] = (window[:, pl.ds(base + HALO, 256)] + total).astype(BF)

    def close_ends(buffer):
        @pl.when(me == 0)
        def _():
            buffer[:, 0:HALO] = jnp.zeros((CH, HALO), F32)

        @pl.when(me == DEVICES - 1)
        def _():
            buffer[:, EXT - HALO : EXT] = jnp.zeros((CH, HALO), F32)

    def layer(buffer, first, do_block):
        copies = ocean_rims(buffer, first)
        for copy in copies:
            copy.start()

        def middle(block, carry):
            do_block(block)
            return carry

        lax.fori_loop(1, 7, middle, 0)
        for copy in copies:
            copy.wait()
        close_ends(buffer)

        def ends(step, carry):
            do_block(step * 7)
            return carry

        lax.fori_loop(0, 2, ends, 0)

    layer(window, 0, hidden_block)
    layer(hwindow, 2, last_block)

    pltpu.make_async_copy(vsend.at[pl.ds(0, DEVICES - 1)], vsend.at[pl.ds(0, DEVICES - 1)], a_send).wait()
    pltpu.make_async_copy(gsend.at[pl.ds(0, DEVICES - 1)], gsend.at[pl.ds(0, DEVICES - 1)], g_send).wait()


def shards(atmos, ocean, heat, w1, w2, m1, m2, slot, cells, taps):
    vmem = pl.BlockSpec(memory_space=pltpu.VMEM)
    dma = pltpu.SemaphoreType.DMA
    air = jnp.transpose(atmos, (1, 0, 2))
    air_next, ocean_next = pl.pallas_call(
        kernel,
        out_shape=(
            jax.ShapeDtypeStruct((AR, CH, AC), BF),
            jax.ShapeDtypeStruct((CH, OCN), BF),
        ),
        in_specs=[vmem] * 10,
        out_specs=(vmem, vmem),
        scratch_shapes=[
            pltpu.VMEM((DEVICES, 1, 128), F32),
            pltpu.VMEM((DEVICES, 1, 128), F32),
            pltpu.VMEM((2, CH, 128), BF),
            pltpu.VMEM((6, CH, 128), BF),
            pltpu.VMEM((2, 2, CH, AC), BF),
            pltpu.VMEM((40, 768), F32),
            pltpu.VMEM((AR + 4, CH, RING), BF),
            pltpu.VMEM((AR + 2, CH, RING), BF),
            pltpu.VMEM((2, CH, RING), F32),
            pltpu.VMEM((2, 3 * CH, 3 * CH), BF),
            pltpu.VMEM((2 * CAP, SLOTS), BF),
            pltpu.VMEM((2, CAP, 128), F32),
            pltpu.VMEM((AC, SLOTS), BF),
            pltpu.VMEM((DEVICES, 16, 128), BF),
            pltpu.VMEM((DEVICES, 16, 128), BF),
            pltpu.VMEM((128, OCN), BF),
            pltpu.VMEM((OCN, OCN), BF),
            pltpu.VMEM((2, CH, TAPS * CH), BF),
            pltpu.VMEM((CH, EXT), F32),
            pltpu.VMEM((CH, EXT), F32),
            pltpu.VMEM((TAPS * CH, 256), BF),
            dma, dma, dma((8,)), dma((8,)), dma((8,)), dma((8,)), dma, dma, dma((4,)), dma((4,)),
        ],
        compiler_params=pltpu.CompilerParams(
            collective_id=0, has_side_effects=True, vmem_limit_bytes=56 << 20
        ),
        name="level",
    )(air, ocean, heat.reshape(1, CH), w1, w2, m1, m2, slot.reshape(1, OCN), cells, taps)
    return jnp.transpose(air_next, (1, 0, 2)), ocean_next


def solution(mesh):
    placed = (
        P(None, "tile", "face"),
        P(None, ("face", "tile")),
        P(),
        P(),
        P(),
        P(),
        P(),
        P(("face", "tile")),
        P(("face", "tile"), None),
        P(None, ("face", "tile")),
    )
    return jax.shard_map(
        shards,
        mesh=mesh,
        in_specs=placed,
        out_specs=(P(None, "tile", "face"), P(None, ("face", "tile"))),
        check_vma=False,
    )
```

profile of v0, /device:TPU:0, one launch (start us, length us, event | category | flops | bytes accessed | tf_op | source)
XLA Modules:
  0.0 93.1 jit_solution(233927459683013048)
XLA Ops:
  0.6 3.0 %copy.15 = bf16[64,24,512]{2,0,1:T(8,128)(2,1)} copy(bf16[64,24,512]{2,1,0:T(8,128)(2,1)} %param.10) | data formatting | bytes 3145728 | tf_op args[0]
  3.7 85.3 %level.1 = (bf16[24,64,512]{2,1,0:T(8,128)(2,1)}, bf16[64,2048]{1,0:T(8,128)(2,1)}) custom-call(bf16[24,64,512]{2,1,0:T(8,128)(2,1)} %bitcast.6, bf16[64,2048]{1,0:T(8,128)(2,1)} %ocean.1, f32[1,64]{1,0:T(1,128)} %bitcast.9, bf16[3,3,64,64]{3,2,1,0:T(8,128)(2,1)} %w1.1, bf16[3,3,64,64]{3,2,1,0:T(8,128)(2,1)} %w2.1, bf16[9,64,64]{2,1,0:T(8,128)(2,1)} %m1.1, ...), custom_call_target="tpu_custom_call" | custom-call | tf_op jit(solution)/shard_map/level/pallas_call | solution.py:410
  89.0 0.0 copy-start
  89.0 3.5 %copy.13 = bf16[64,24,512]{2,1,0:T(8,128)(2,1)} copy(bf16[64,24,512]{2,0,1:T(8,128)(2,1)} %bitcast.7) | data formatting | bytes 3145728
  92.4 0.0 copy-done
  92.4 0.7 copy.17
Async XLA Ops:
  89.0 3.5 %copy-start = (bf16[64,2048]{1,0:T(8,128)(2,1)S(1)}, bf16[64,2048]{1,0:T(8,128)(2,1)}, u32[]{:S(2)}) copy-start(bf16[64,2048]{1,0:T(8,128)(2,1)} %get-tuple-element.11) | copy-start | bytes 786436
where the time goes:
time: 93.3 us; the launch traced here: 93.1 us
  Pallas kernels  85.3 us (91%)
  local copies, waits for them, and re-layouts  7.21 us (8%)
    pallas_call x1, Pallas kernels, shards(): pl.pallas_call(kernel, out_shape=(jax.ShapeDtypeStruct((AR, CH, AC), BF),...  85.3 us
    unnamed x5, local copies, waits for them, and re-layouts  7.21 us

commit v1 on v0

--- a/solution.py
+++ b/solution.py
@@ -47,9 +47,10 @@
 def kernel(
     air, ocean, heat, w1, w2, m1, m2, slot, cells, taps,
     air_out, ocean_out,
-    vsend, vrecv, cols, rcols, rrows, sst, sx, hx, acc, weights, picked_cols, table, onecol,
-    gsend, grecv, arrived, oneslot, mweights, window, hwindow, picked,
-    a_send, a_recv, r_send, r_recv, s_send, s_recv, g_send, g_recv, o_send, o_recv,
+    air_in, w1_in, w2_in, m1_in, m2_in, taps_in, air_done, after,
+    vsend, vrecv, cols, rcols, sst, sx, hx, acc, weights, picked_cols, table, onecol,
+    gsend, grecv, arrived, oneslot, onetap, mweights, window, hwindow,
+    local, a_send, a_recv, r_send, r_recv, s_send, s_recv, g_send, g_recv, o_send, o_recv,
 ):
     face = lax.axis_index("face")
     tile = lax.axis_index("tile")
@@ -63,6 +64,15 @@
         return carry
 
     lax.fori_loop(1, DEVICES, greet, 0)
+
+    loads = [
+        pltpu.make_async_copy(src, dst, local.at[number])
+        for number, (src, dst) in enumerate(
+            ((air, air_in), (w1, w1_in), (w2, w2_in), (m1, m1_in), (m2, m2_in), (taps, taps_in))
+        )
+    ]
+    for copy in loads:
+        copy.start()
 
     slots = slot[...]
     heat_row = ocean[0:16, :].astype(F32)[0:1]
@@ -73,21 +83,6 @@
     values = jnp.where(place == position + CAP, 1.0, values).astype(BF)
     vsend[:, 0, :] = dot_nt(source, values)
 
-    lane = iota((CH, 128), 1)
-
-    def pack_row(row, carry):
-        left, right = carry
-        first = jnp.where(lane < 2, air[row, :, 0:128].astype(F32), 0.0)
-        last = jnp.where(lane >= 126, air[row, :, AC - 128 : AC].astype(F32), 0.0)
-        left = left + pltpu.roll(first, 2 * row, 1)
-        right = right + pltpu.roll(last, 2 * row + 2, 1)
-        return left, right
-
-    zero = jnp.zeros((CH, 128), F32)
-    left, right = lax.fori_loop(0, AR, pack_row, (zero, zero))
-    cols[0] = left.astype(BF)
-    cols[1] = right.astype(BF)
-
     pl.semaphore_wait(barrier, DEVICES - 1)
 
     def send_values(step, carry):
@@ -100,6 +95,25 @@
 
     lax.fori_loop(1, DEVICES, send_values, 0)
     vrecv[me] = vsend[me]
+
+    for copy in loads:
+        copy.wait()
+    sx[2 : AR + 2, :, 0:AC] = pltpu.einshape("crw->rcw", air_in[...])
+
+    lane = iota((CH, 128), 1)
+
+    def pack_row(row, carry):
+        left, right = carry
+        first = jnp.where(lane < 2, sx[row + 2, :, 0:128].astype(F32), 0.0)
+        last = jnp.where(lane >= 126, sx[row + 2, :, AC - 128 : AC].astype(F32), 0.0)
+        left = left + pltpu.roll(first, 2 * row, 1)
+        right = right + pltpu.roll(last, 2 * row + 2, 1)
+        return left, right
+
+    zero = jnp.zeros((CH, 128), F32)
+    left, right = lax.fori_loop(0, AR, pack_row, (zero, zero), unroll=6)
+    cols[0] = left.astype(BF)
+    cols[1] = right.astype(BF)
 
     up = lax.rem(tile + TILES - 1, TILES)
     down = lax.rem(tile + 1, TILES)
@@ -117,8 +131,8 @@
         )
 
     air_rims = [
-        rim(0, air.at[0:2], rrows.at[1], r_send, r_recv),
-        rim(1, air.at[AR - 2 : AR], rrows.at[0], r_send, r_recv),
+        rim(0, sx.at[2:4, :, 0:AC], sx.at[AR + 2 : AR + 4, :, 0:AC], r_send, r_recv),
+        rim(1, sx.at[AR : AR + 2, :, 0:AC], sx.at[0:2, :, 0:AC], r_send, r_recv),
         rim(2, cols.at[0], rcols.at[1], r_send, r_recv),
         rim(3, cols.at[1], rcols.at[0], r_send, r_recv),
         rim(4, cols.at[0], rcols.at[5], r_send, r_recv),
@@ -135,14 +149,14 @@
         onecol[:, pl.ds(base, 256)] = onehot(iota((AC, 256), 0) == column)
         return carry
 
-    lax.fori_loop(0, SLOTS // 256, make_columns, 0)
-    for number, weight in enumerate((w1, w2)):
+    lax.fori_loop(0, SLOTS // 256, make_columns, 0, unroll=2)
+    for number, weight in enumerate((w1_in, w2_in)):
         for row_tap in range(3):
             for col_tap in range(3):
                 weights[number, row_tap * CH : (row_tap + 1) * CH, col_tap * CH : (col_tap + 1) * CH] = weight[
                     row_tap, col_tap
                 ]
-    for number, weight in enumerate((m1, m2)):
+    for number, weight in enumerate((m1_in, m2_in)):
         for tap in range(TAPS):
             mweights[number, :, tap * CH : (tap + 1) * CH] = weight[tap]
     channel_weight = jnp.sum(
@@ -158,15 +172,12 @@
         return jnp.where(lane < 64, from_right, from_left).astype(BF)
 
     def extend(row, carry):
-        sx[row + 2, :, 0:AC] = air[row]
         sx[row + 2, :, AC:RING] = ring_block(row, rcols[0].astype(F32), rcols[1].astype(F32))
         return carry
 
-    lax.fori_loop(0, AR, extend, 0)
+    lax.fori_loop(0, AR, extend, 0, unroll=6)
     for row in range(2):
-        sx[row, :, 0:AC] = rrows[0, row]
         sx[row, :, AC:RING] = ring_block(jnp.int32(AR - 2 + row), rcols[2].astype(F32), rcols[3].astype(F32))
-        sx[AR + 2 + row, :, 0:AC] = rrows[1, row]
         sx[AR + 2 + row, :, AC:RING] = ring_block(jnp.int32(row), rcols[4].astype(F32), rcols[5].astype(F32))
 
     pltpu.make_async_copy(vrecv.at[pl.ds(0, DEVICES - 1)], vrecv.at[pl.ds(0, DEVICES - 1)], a_recv).wait()
@@ -189,7 +200,7 @@
             ).astype(BF)
         return carry
 
-    lax.fori_loop(0, SLOTS // 128, make_rows, 0)
+    lax.fori_loop(0, SLOTS // 128, make_rows, 0, unroll=8)
     sums = dot_nt(picked_cols[...], onecol[...])
     sst[8 : 8 + AR, 128 : 128 + AC] = sums[0:AR] / jnp.maximum(sums[CAP : CAP + AR], 1.0)
 
@@ -221,13 +232,12 @@
         sx[row] = jnp.where(inside, state, 0.0).astype(BF)
         return carry
 
-    lax.fori_loop(0, AR + 4, begin, 0)
+    lax.fori_loop(0, AR + 4, begin, 0, unroll=7)
 
     def three(x, width):
-        wide = x.astype(F32)
-        before = pltpu.roll(wide, 1, 1).astype(BF)[:, 0:width]
-        after = pltpu.roll(wide, RING - 1, 1).astype(BF)[:, 0:width]
-        return jnp.concatenate([before, x[:, 0:width], after], axis=0)
+        west_of = pltpu.roll(x, 1, 1)[:, 0:width]
+        east_of = pltpu.roll(x, RING - 1, 1)[:, 0:width]
+        return jnp.concatenate([west_of, x[:, 0:width], east_of], axis=0)
 
     def first_conv(row, carry):
         part = dot(weights[0], three(sx[row], RING))
@@ -240,7 +250,7 @@
         hx[jnp.maximum(middle, 0)] = hidden.astype(BF)
         return carry
 
-    lax.fori_loop(0, AR + 4, first_conv, 0)
+    lax.fori_loop(0, AR + 4, first_conv, 0, unroll=AR + 4)
 
     def second_conv(row, carry):
         part = dot(weights[1], three(hx[row], AC))
@@ -248,39 +258,51 @@
         acc[0, :, 0:AC] = acc[1, :, 0:AC] + part[CH : 2 * CH]
         acc[1, :, 0:AC] = part[0:CH]
         middle = jnp.maximum(row - 2, 0)
-        air_out[middle] = (sx[middle + 2, :, 0:AC].astype(F32) + total).astype(BF)
-        return carry
-
-    lax.fori_loop(0, AR + 2, second_conv, 0)
-
-    def coupling(step, carry):
-        block = lax.rem(lax.div(me, 8) + step, DEVICES // 8)
+        after[middle] = (sx[middle + 2, :, 0:AC].astype(F32) + total).astype(BF)
+        return carry
+
+    lax.fori_loop(0, AR + 2, second_conv, 0, unroll=AR + 2)
+
+    first_block = lax.div(me, 8)
+
+    def block_of(step):
+        return lax.rem(first_block + step, DEVICES // 8)
+
+    def find(block):
         base = pl.multiple_of(block * 256, 256)
         row = cells[0:1, pl.ds(base, 256)] // AC
         select = onecol[:, pl.ds(base, 256)]
         state = jnp.zeros((CH, 256), F32)
         for part in range(AR // 4):
-            rows = air_out[part * 4 : part * 4 + 4].reshape(4 * CH, AC)
+            rows = after[part * 4 : part * 4 + 4].reshape(4 * CH, AC)
             found = dot(rows, select)
             for inner in range(4):
                 state = jnp.where(row == part * 4 + inner, found[inner * CH : (inner + 1) * CH], state)
+        return state
+
+    def ship(state, block, others):
         flat = jnp.transpose(state).reshape(8, CAP, CH)
         pair = jnp.concatenate([flat[:, 0:16], flat[:, 16:32]], axis=2)
         gsend[pl.ds(pl.multiple_of(block * 8, 8), 8)] = pair.astype(BF)
-        for inner in range(8):
+        for inner in others:
             other = block * 8 + inner
-
-            @pl.when(other != me)
-            def _():
-                pltpu.make_async_remote_copy(
-                    src_ref=gsend.at[other], dst_ref=grecv.at[me], send_sem=g_send, recv_sem=g_recv,
-                    device_id=where_of(other), device_id_type=MESH,
-                ).start()
-
-        return carry
-
-    lax.fori_loop(0, DEVICES // 8, coupling, 0)
+            pltpu.make_async_remote_copy(
+                src_ref=gsend.at[other], dst_ref=grecv.at[me], send_sem=g_send, recv_sem=g_recv,
+                device_id=where_of(other), device_id_type=MESH,
+            ).start()
+
+    def coupling(step, state):
+        found = find(block_of(step))
+        ship(state, block_of(step - 1), range(8))
+        return found
+
+    state = lax.fori_loop(2, DEVICES // 8 + 1, coupling, find(block_of(1)), unroll=3)
+    ship(state, first_block, [lax.rem(me + step, 8) for step in range(1, 8)])
     grecv[me] = gsend[me]
+
+    air_done[...] = pltpu.einshape("rcw->crw", after[...])
+    store = pltpu.make_async_copy(air_done, air_out, local.at[0])
+    store.start()
 
     def make_slots(step, carry):
         base = pl.multiple_of(step * 256, 256)
@@ -295,6 +317,15 @@
         return lax.fori_loop(0, OCN // 256, fill, carry)
 
     lax.fori_loop(0, OCN // 256, make_slots, 0)
+
+    def make_taps(step, carry):
+        base = pl.multiple_of(step * 256, 256)
+        for tap in range(TAPS):
+            inner = (taps_in[tap : tap + 1, pl.ds(base, 256)] - base) % 256
+            onetap[tap, :, pl.ds(base, 256)] = onehot(iota((256, 256), 0) == inner)
+        return carry
+
+    lax.fori_loop(0, OCN // 256, make_taps, 0)
     pltpu.make_async_copy(grecv.at[pl.ds(0, DEVICES - 1)], grecv.at[pl.ds(0, DEVICES - 1)], g_recv).wait()
 
     def turn(step, carry):
@@ -302,7 +333,7 @@
         arrived[:, pl.ds(pl.multiple_of(step * 128, 128), 128)] = jnp.transpose(eight.astype(F32)).astype(BF)
         return carry
 
-    lax.fori_loop(0, DEVICES // 8, turn, 0)
+    lax.fori_loop(0, DEVICES // 8, turn, 0, unroll=8)
 
     def force(step, carry):
         base = pl.multiple_of(step * 256, 256)
@@ -310,71 +341,59 @@
         found = dot(arrived[...], oneslot[:, pl.ds(base, 256)])
         forcing = jnp.where(late, found[CH : 2 * CH], found[0:CH])
         begun = ocean[:, pl.ds(base, 256)].astype(F32) + forcing
-        window[:, pl.ds(base + HALO, 256)] = begun.astype(BF).astype(F32)
-        return carry
-
-    lax.fori_loop(0, OCN // 256, force, 0)
-
-    before = where_of(lax.rem(me + DEVICES - 1, DEVICES))
-    after = where_of(lax.rem(me + 1, DEVICES))
+        window[:, pl.ds(base + HALO, 256)] = begun.astype(BF)
+        return carry
+
+    lax.fori_loop(0, OCN // 256, force, 0, unroll=4)
+
+    previous = where_of(lax.rem(me + DEVICES - 1, DEVICES))
+    following = where_of(lax.rem(me + 1, DEVICES))
 
     def ocean_rims(buffer, first):
         return [
             pltpu.make_async_remote_copy(
                 src_ref=buffer.at[:, HALO : 2 * HALO], dst_ref=buffer.at[:, EXT - HALO : EXT],
-                send_sem=o_send.at[first], recv_sem=o_recv.at[first], device_id=before, device_id_type=MESH,
+                send_sem=o_send.at[first], recv_sem=o_recv.at[first], device_id=previous, device_id_type=MESH,
             ),
             pltpu.make_async_remote_copy(
                 src_ref=buffer.at[:, OCN : OCN + HALO], dst_ref=buffer.at[:, 0:HALO],
-                send_sem=o_send.at[first + 1], recv_sem=o_recv.at[first + 1], device_id=after, device_id_type=MESH,
+                send_sem=o_send.at[first + 1], recv_sem=o_recv.at[first + 1], device_id=following, device_id_type=MESH,
             ),
         ]
 
     def mix(buffer, number, block):
-        for half in range(2):
-            base = pl.multiple_of(block * 256 + half * 128, 128)
-            parts = [
-                [
-                    buffer[group * 8 : (group + 1) * 8, pl.ds(pl.multiple_of(base + part * 128, 128), 128)]
-                    for part in range(5)
-                ]
-                for group in range(CH // 8)
-            ]
-            for tap in range(TAPS):
-                index = jnp.broadcast_to(taps[tap : tap + 1, pl.ds(base, 128)] - base, (8, 128))
-                inner = index % 128
-                part_of = index // 128
-                groups = []
-                for group in range(CH // 8):
-                    found = jnp.take_along_axis(parts[group][0], inner, axis=1)
-                    for part in range(1, 5):
-                        found = jnp.where(
-                            part_of == part, jnp.take_along_axis(parts[group][part], inner, axis=1), found
-                        )
-                    groups.append(found)
-                picked[tap * CH : (tap + 1) * CH, half * 128 : (half + 1) * 128] = jnp.concatenate(
-                    groups, axis=0
-                ).astype(BF)
-        return dot(mweights[number], picked[...])
+        base = pl.multiple_of(block * 256, 256)
+        segments = jnp.concatenate(
+            [buffer[:, pl.ds(pl.multiple_of(base + 256 * part, 256), 256)] for part in range(3)], axis=0
+        )
+        groups = []
+        for tap in range(TAPS):
+            part_of = (taps_in[tap : tap + 1, pl.ds(base, 256)] - base) // 256
+            found = dot(segments, onetap[tap, :, pl.ds(base, 256)])
+            chosen = jnp.where(
+                part_of == 0, found[0:CH], jnp.where(part_of == 1, found[CH : 2 * CH], found[2 * CH : 3 * CH])
+            )
+            groups.append(chosen.astype(BF))
+        return dot(mweights[number], jnp.concatenate(groups, axis=0))
 
     def hidden_block(block):
         total = mix(window, 0, block)
         base = pl.multiple_of(block * 256, 256)
-        hwindow[:, pl.ds(base + HALO, 256)] = jax.nn.gelu(total, approximate=True).astype(BF).astype(F32)
+        hwindow[:, pl.ds(base + HALO, 256)] = jax.nn.gelu(total, approximate=True).astype(BF)
 
     def last_block(block):
         total = mix(hwindow, 1, block)
         base = pl.multiple_of(block * 256, 256)
-        ocean_out[:, pl.ds(base, 256)] = (window[:, pl.ds(base + HALO, 256)] + total).astype(BF)
+        ocean_out[:, pl.ds(base, 256)] = (window[:, pl.ds(base + HALO, 256)].astype(F32) + total).astype(BF)
 
     def close_ends(buffer):
         @pl.when(me == 0)
         def _():
-            buffer[:, 0:HALO] = jnp.zeros((CH, HALO), F32)
+            buffer[:, 0:HALO] = jnp.zeros((CH, HALO), BF)
 
         @pl.when(me == DEVICES - 1)
         def _():
-            buffer[:, EXT - HALO : EXT] = jnp.zeros((CH, HALO), F32)
+            buffer[:, EXT - HALO : EXT] = jnp.zeros((CH, HALO), BF)
 
     def layer(buffer, first, do_block):
         copies = ocean_rims(buffer, first)
@@ -385,7 +404,7 @@
             do_block(block)
             return carry
 
-        lax.fori_loop(1, 7, middle, 0)
+        lax.fori_loop(1, 7, middle, 0, unroll=6)
         for copy in copies:
             copy.wait()
         close_ends(buffer)
@@ -394,33 +413,57 @@
             do_block(step * 7)
             return carry
 
-        lax.fori_loop(0, 2, ends, 0)
+        lax.fori_loop(0, 2, ends, 0, unroll=2)
 
     layer(window, 0, hidden_block)
     layer(hwindow, 2, last_block)
+    store.wait()
 
     pltpu.make_async_copy(vsend.at[pl.ds(0, DEVICES - 1)], vsend.at[pl.ds(0, DEVICES - 1)], a_send).wait()
     pltpu.make_async_copy(gsend.at[pl.ds(0, DEVICES - 1)], gsend.at[pl.ds(0, DEVICES - 1)], g_send).wait()
+
+
+def hand_over(air, ocean, air_out, ocean_out, air_held, ocean_held, come, go):
+    pieces = [(ocean, ocean_held, ocean_out)]
+    for part in range(4):
+        rows = pl.ds(part * 16, 16)
+        pieces.append((air.at[rows], air_held.at[rows], air_out.at[rows]))
+    inward = [pltpu.make_async_copy(src, held, come.at[i]) for i, (src, held, _) in enumerate(pieces)]
+    outward = [pltpu.make_async_copy(held, dst, go.at[i]) for i, (_, held, dst) in enumerate(pieces)]
+    for copy in inward:
+        copy.start()
+    for first, second in zip(inward, outward):
+        first.wait()
+        second.start()
+    for copy in outward:
+        copy.wait()
 
 
 def shards(atmos, ocean, heat, w1, w2, m1, m2, slot, cells, taps):
     vmem = pl.BlockSpec(memory_space=pltpu.VMEM)
     dma = pltpu.SemaphoreType.DMA
-    air = jnp.transpose(atmos, (1, 0, 2))
-    air_next, ocean_next = pl.pallas_call(
+    anywhere = pl.BlockSpec(memory_space=pl.ANY)
+    results = pl.pallas_call(
         kernel,
         out_shape=(
-            jax.ShapeDtypeStruct((AR, CH, AC), BF),
+            jax.ShapeDtypeStruct((CH, AR, AC), BF),
             jax.ShapeDtypeStruct((CH, OCN), BF),
         ),
-        in_specs=[vmem] * 10,
-        out_specs=(vmem, vmem),
+        in_specs=[anywhere, vmem, vmem] + [anywhere] * 4 + [vmem, vmem, anywhere],
+        out_specs=(anywhere, vmem),
         scratch_shapes=[
+            pltpu.VMEM((CH, AR, AC), BF),
+            pltpu.VMEM((3, 3, CH, CH), BF),
+            pltpu.VMEM((3, 3, CH, CH), BF),
+            pltpu.VMEM((TAPS, CH, CH), BF),
+            pltpu.VMEM((TAPS, CH, CH), BF),
+            pltpu.VMEM((TAPS, OCN), I32),
+            pltpu.VMEM((CH, AR, AC), BF),
+            pltpu.VMEM((AR, CH, AC), BF),
             pltpu.VMEM((DEVICES, 1, 128), F32),
             pltpu.VMEM((DEVICES, 1, 128), F32),
             pltpu.VMEM((2, CH, 128), BF),
             pltpu.VMEM((6, CH, 128), BF),
-            pltpu.VMEM((2, 2, CH, AC), BF),
             pltpu.VMEM((40, 768), F32),
             pltpu.VMEM((AR + 4, CH, RING), BF),
             pltpu.VMEM((AR + 2, CH, RING), BF),
@@ -433,18 +476,28 @@
             pltpu.VMEM((DEVICES, 16, 128), BF),
             pltpu.VMEM((128, OCN), BF),
             pltpu.VMEM((OCN, OCN), BF),
+            pltpu.VMEM((TAPS, 256, OCN), BF),
             pltpu.VMEM((2, CH, TAPS * CH), BF),
-            pltpu.VMEM((CH, EXT), F32),
-            pltpu.VMEM((CH, EXT), F32),
-            pltpu.VMEM((TAPS * CH, 256), BF),
-            dma, dma, dma((8,)), dma((8,)), dma((8,)), dma((8,)), dma, dma, dma((4,)), dma((4,)),
+            pltpu.VMEM((CH, EXT), BF),
+            pltpu.VMEM((CH, EXT), BF),
+            dma((6,)), dma, dma, dma((8,)), dma((8,)), dma((8,)), dma((8,)), dma, dma, dma((4,)), dma((4,)),
         ],
         compiler_params=pltpu.CompilerParams(
             collective_id=0, has_side_effects=True, vmem_limit_bytes=56 << 20
         ),
         name="level",
-    )(air, ocean, heat.reshape(1, CH), w1, w2, m1, m2, slot.reshape(1, OCN), cells, taps)
-    return jnp.transpose(air_next, (1, 0, 2)), ocean_next
+    )(atmos, ocean, heat.reshape(1, CH), w1, w2, m1, m2, slot.reshape(1, OCN), cells, taps)
+    return pl.pallas_call(
+        hand_over,
+        out_shape=(
+            jax.ShapeDtypeStruct((CH, AR, AC), BF),
+            jax.ShapeDtypeStruct((CH, OCN), BF),
+        ),
+        in_specs=[anywhere, anywhere],
+        out_specs=(anywhere, anywhere),
+        scratch_shapes=[pltpu.VMEM((CH, AR, AC), BF), pltpu.VMEM((CH, OCN), BF), dma((5,)), dma((5,))],
+        name="hand_over",
+    )(*results)
 
 
 def solution(mesh):

time: 93.3 us -> 67.3 us (0.72)
  Pallas kernels: 85.3 us -> 66.3 us
  local copies, waits for them, and re-layouts: 7.21 us -> 0 us
    pallas_call x1 -> x2, Pallas kernels: 85.3 us -> 66.3 us  [the longest x1 64 us: shards(): pl.pallas_call(kernel, out_shape=(jax.ShapeDtypeStruct((CH, AR, AC), BF),...]
    unnamed x5 -> x0, local copies, waits for them, and re-layouts: 7.21 us -> none
where the time goes in v1:
time: 67.3 us; the launch traced here: 67.1 us
  Pallas kernels  66.3 us (99%)
  between operations  0.8 us (1%)
    pallas_call x1, Pallas kernels, shards(): pl.pallas_call(kernel, out_shape=(jax.ShapeDtypeStruct((CH, AR, AC), BF),...  64 us
    pallas_call x1, Pallas kernels, shards(): pl.pallas_call(hand_over, out_shape=(jax.ShapeDtypeStruct((CH, AR, AC), B...  2.3 us

profile of v1, /device:TPU:0, one launch (start us, length us, event | category | flops | bytes accessed | tf_op | source)
XLA Modules:
  0.0 67.1 jit_solution(3761974680965490318)
XLA Ops:
  0.6 64.0 %level.1 = (bf16[64,24,512]{2,1,0:T(8,128)(2,1)}, bf16[64,2048]{1,0:T(8,128)(2,1)}) custom-call(bf16[64,24,512]{2,1,0:T(8,128)(2,1)} %air.1, bf16[64,2048]{1,0:T(8,128)(2,1)} %ocean.1, f32[1,64]{1,0:T(1,128)} %bitcast.3, bf16[3,3,64,64]{3,2,1,0:T(8,128)(2,1)} %w1.1, bf16[3,3,64,64]{3,2,1,0:T(8,128)(2,1)} %w2.1, bf16[9,64,64]{2,1,0:T(8,128)(2,1)} %m1.1, ...), custom_call_target="tpu_custom_call" | custom-call | tf_op jit(solution)/shard_map/level/pallas_call | solution.py:446
  64.7 2.3 %hand_over.1 = (bf16[64,24,512]{2,1,0:T(8,128)(2,1)}, bf16[64,2048]{1,0:T(8,128)(2,1)}) custom-call(bf16[64,24,512]{2,1,0:T(8,128)(2,1)} %get-tuple-element.4.air, bf16[64,2048]{1,0:T(8,128)(2,1)} %get-tuple-element.5.ocean), custom_call_target="tpu_custom_call" | custom-call | tf_op jit(solution)/shard_map/hand_over/pallas_call | solution.py:490

commit v2 on v1

--- a/solution.py
+++ b/solution.py
@@ -48,22 +48,37 @@
     air, ocean, heat, w1, w2, m1, m2, slot, cells, taps,
     air_out, ocean_out,
     air_in, w1_in, w2_in, m1_in, m2_in, taps_in, air_done, after,
-    vsend, vrecv, cols, rcols, sst, sx, hx, acc, weights, picked_cols, table, onecol,
+    vsend, vfirst, vturned, vrecv, cols, rcols, sst, sx, hx, acc, weights, picked_cols, onecol,
     gsend, grecv, arrived, oneslot, onetap, mweights, window, hwindow,
-    local, a_send, a_recv, r_send, r_recv, s_send, s_recv, g_send, g_recv, o_send, o_recv,
+    local, a_send, a_recv, b_send, b_recv, r_send, r_recv, s_send, s_recv, g_send, g_recv, o_send, o_recv,
 ):
     face = lax.axis_index("face")
     tile = lax.axis_index("tile")
     me = face * TILES + tile
 
+    outer = face * 2 + lax.div(tile, 16)
+    inner_place = lax.rem(tile, 16)
+    up = lax.rem(tile + TILES - 1, TILES)
+    down = lax.rem(tile + 1, TILES)
+    west = lax.rem(face + FACES - 1, FACES)
+    east = lax.rem(face + 1, FACES)
+    around = (
+        (face, up), (face, down), (west, tile), (east, tile),
+        (west, up), (west, down), (east, up), (east, down),
+    )
+
+    def outer_peer(number):
+        return (lax.div(number, 2), lax.rem(number, 2) * 16 + inner_place)
+
+    def inner_peer(number):
+        return (face, lax.div(tile, 16) * 16 + number)
+
     barrier = pltpu.get_barrier_semaphore()
-
-    def greet(step, carry):
-        other = lax.rem(me + step, DEVICES)
-        pl.semaphore_signal(barrier, inc=1, device_id=where_of(other), device_id_type=MESH)
-        return carry
-
-    lax.fori_loop(1, DEVICES, greet, 0)
+    greeted = [outer_peer(lax.rem(outer + step, 8)) for step in range(1, 8)]
+    greeted += [inner_peer(lax.rem(inner_place + step, 16)) for step in range(1, 16)]
+    greeted += list(around)
+    for other in greeted:
+        pl.semaphore_signal(barrier, inc=1, device_id=other, device_id_type=MESH)
 
     loads = [
         pltpu.make_async_copy(src, dst, local.at[number])
@@ -77,24 +92,18 @@
     slots = slot[...]
     heat_row = ocean[0:16, :].astype(F32)[0:1]
     source = onehot(iota((DEVICES, OCN), 0) == slots // CAP)
-    place = iota((DEVICES, OCN), 0)
-    position = slots % CAP
-    values = jnp.where(place == position, heat_row, 0.0)
-    values = jnp.where(place == position + CAP, 1.0, values).astype(BF)
-    vsend[:, 0, :] = dot_nt(source, values)
-
-    pl.semaphore_wait(barrier, DEVICES - 1)
-
-    def send_values(step, carry):
-        other = lax.rem(me + step, DEVICES)
+    here = iota((128, OCN), 0) == slots % CAP + CAP * lax.rem(me, 4)
+    values = jnp.concatenate([jnp.where(here, heat_row, 0.0).astype(BF), onehot(here)], axis=0)
+    vsend[...] = dot_nt(source, values).reshape(8, 16, 256)
+
+    pl.semaphore_wait(barrier, len(greeted))
+    for step in range(1, 8):
+        other = lax.rem(outer + step, 8)
         pltpu.make_async_remote_copy(
-            src_ref=vsend.at[other], dst_ref=vrecv.at[me], send_sem=a_send, recv_sem=a_recv,
-            device_id=where_of(other), device_id_type=MESH,
+            src_ref=vsend.at[other], dst_ref=vfirst.at[outer], send_sem=a_send, recv_sem=a_recv,
+            device_id=outer_peer(other), device_id_type=MESH,
         ).start()
-        return carry
-
-    lax.fori_loop(1, DEVICES, send_values, 0)
-    vrecv[me] = vsend[me]
+    vfirst[outer] = vsend[outer]
 
     for copy in loads:
         copy.wait()
@@ -114,15 +123,6 @@
     left, right = lax.fori_loop(0, AR, pack_row, (zero, zero), unroll=6)
     cols[0] = left.astype(BF)
     cols[1] = right.astype(BF)
-
-    up = lax.rem(tile + TILES - 1, TILES)
-    down = lax.rem(tile + 1, TILES)
-    west = lax.rem(face + FACES - 1, FACES)
-    east = lax.rem(face + 1, FACES)
-    around = (
-        (face, up), (face, down), (west, tile), (east, tile),
-        (west, up), (west, down), (east, up), (east, down),
-    )
 
     def rim(number, src, dst, send, recv):
         return pltpu.make_async_remote_copy(
@@ -142,6 +142,16 @@
     ]
     for copy in air_rims:
         copy.start()
+
+    pltpu.make_async_copy(vfirst.at[pl.ds(0, 7)], vfirst.at[pl.ds(0, 7)], a_recv).wait()
+    vturned[...] = pltpu.einshape("bal->abl", vfirst[...])
+    for step in range(1, 16):
+        other = lax.rem(inner_place + step, 16)
+        pltpu.make_async_remote_copy(
+            src_ref=vturned.at[other], dst_ref=vrecv.at[inner_place], send_sem=b_send, recv_sem=b_recv,
+            device_id=inner_peer(other), device_id_type=MESH,
+        ).start()
+    vrecv[inner_place] = vturned[inner_place]
 
     def make_columns(step, carry):
         base = pl.multiple_of(step * 256, 256)
@@ -163,44 +173,17 @@
         jnp.where(iota((CH, CH), 0) == iota((CH, CH), 1), heat[...], 0.0), axis=1, keepdims=True
     )
 
-    for copy in air_rims:
-        copy.wait()
-
-    def ring_block(row, left, right):
-        from_right = pltpu.roll(right, lax.rem(128 - 2 * row, 128), 1)
-        from_left = pltpu.roll(left, lax.rem(254 - 2 * row, 128), 1)
-        return jnp.where(lane < 64, from_right, from_left).astype(BF)
-
-    def extend(row, carry):
-        sx[row + 2, :, AC:RING] = ring_block(row, rcols[0].astype(F32), rcols[1].astype(F32))
-        return carry
-
-    lax.fori_loop(0, AR, extend, 0, unroll=6)
-    for row in range(2):
-        sx[row, :, AC:RING] = ring_block(jnp.int32(AR - 2 + row), rcols[2].astype(F32), rcols[3].astype(F32))
-        sx[AR + 2 + row, :, AC:RING] = ring_block(jnp.int32(row), rcols[4].astype(F32), rcols[5].astype(F32))
-
-    pltpu.make_async_copy(vrecv.at[pl.ds(0, DEVICES - 1)], vrecv.at[pl.ds(0, DEVICES - 1)], a_recv).wait()
-    got = vrecv[:, 0, :].astype(BF)
-    square = (DEVICES, 128)
-    mine = iota(square, 0) % 4 == iota(square, 1) // CAP
-    group = onehot(iota((CAP, DEVICES), 0) == iota((CAP, DEVICES), 1) // 4)
-    for kind in range(2):
-        expand = onehot(iota(square, 0) - CAP * kind == iota(square, 1) % CAP)
-        spread = jnp.where(mine, dot(got, expand), 0.0).astype(BF)
-        table[kind] = dot(group, spread)
-
-    def make_rows(step, carry):
-        base = pl.multiple_of(step * 128, 128)
-        row = cells[0:1, pl.ds(base, 128)] // AC
-        hit = iota((CAP, 128), 0) == row
-        for kind in range(2):
-            picked_cols[CAP * kind : CAP * (kind + 1), pl.ds(base, 128)] = jnp.where(
-                hit, table[kind, pl.ds(step, 1), :], 0.0
-            ).astype(BF)
-        return carry
-
-    lax.fori_loop(0, SLOTS // 128, make_rows, 0, unroll=8)
+    pltpu.make_async_copy(vrecv.at[pl.ds(0, 15)], vrecv.at[pl.ds(0, 15)], b_recv).wait()
+    for quarter in range(4):
+        four = vrecv[quarter * 4 : quarter * 4 + 4]
+        lines = (four[0] + four[1]) + (four[2] + four[3])
+        for part in range(8):
+            base = (part * 4 + quarter) * 128
+            hit = iota((CAP, 128), 0) == cells[0:1, base : base + 128] // AC
+            for kind in range(2):
+                picked_cols[CAP * kind : CAP * (kind + 1), base : base + 128] = jnp.where(
+                    hit, lines[part : part + 1, kind * 128 : (kind + 1) * 128], 0.0
+                ).astype(BF)
     sums = dot_nt(picked_cols[...], onecol[...])
     sst[8 : 8 + AR, 128 : 128 + AC] = sums[0:AR] / jnp.maximum(sums[CAP : CAP + AR], 1.0)
 
@@ -217,22 +200,60 @@
     ]
     for copy in sst_rims:
         copy.start()
+    def begin(row, carry):
+        line = sst[pl.ds(row + 8, 1), 128 : 128 + AC]
+        state = sx[row + 2, :, 0:AC].astype(F32) + channel_weight * line
+        sx[row + 2, :, 0:AC] = state.astype(BF)
+        return carry
+
+    for copy in air_rims:
+        copy.wait()
+    lax.fori_loop(0, AR, begin, 0, unroll=6)
+
+    def ring_block(row, left, right):
+        from_right = pltpu.roll(right, lax.rem(128 - 2 * row, 128), 1)
+        from_left = pltpu.roll(left, lax.rem(254 - 2 * row, 128), 1)
+        return jnp.where(lane < 64, from_right, from_left).astype(BF)
+
+    def extend(row, carry):
+        sx[row + 2, :, AC:RING] = ring_block(row, rcols[0].astype(F32), rcols[1].astype(F32))
+        return carry
+
+    lax.fori_loop(0, AR, extend, 0, unroll=6)
+    for row in range(2):
+        sx[row, :, AC:RING] = ring_block(jnp.int32(AR - 2 + row), rcols[2].astype(F32), rcols[3].astype(F32))
+        sx[AR + 2 + row, :, AC:RING] = ring_block(jnp.int32(row), rcols[4].astype(F32), rcols[5].astype(F32))
+
+    def make_taps(step, carry):
+        base = pl.multiple_of(step * 256, 256)
+        for tap in range(TAPS):
+            inner = (taps_in[tap : tap + 1, pl.ds(base, 256)] - base) % 256
+            onetap[tap, :, pl.ds(base, 256)] = onehot(iota((256, 256), 0) == inner)
+        return carry
+
+    lax.fori_loop(0, OCN // 256, make_taps, 0)
+
     for copy in sst_rims:
         copy.wait()
 
     low_lane = iota((1, 128), 1) < 64
 
-    def begin(row, carry):
-        line = sst[pl.ds(row + 6, 1), :]
-        ring = jnp.concatenate(
-            [line[:, 128 : 128 + AC], jnp.where(low_lane, line[:, 640:768], line[:, 0:128])], axis=1
-        )
-        state = sx[row].astype(F32) + channel_weight * ring
-        inside = jnp.logical_and(jnp.logical_or(row >= 2, tile > 0), jnp.logical_or(row < AR + 2, tile < TILES - 1))
-        sx[row] = jnp.where(inside, state, 0.0).astype(BF)
-        return carry
-
-    lax.fori_loop(0, AR + 4, begin, 0, unroll=7)
+    def begin_block(row, inside):
+        whole = sst[pl.ds(row + 6, 1), :]
+        line = jnp.where(low_lane, whole[:, 640:768], whole[:, 0:128])
+        state = sx[row, :, AC:RING].astype(F32) + channel_weight * line
+        sx[row, :, AC:RING] = jnp.where(inside, state, 0.0).astype(BF)
+
+    def begin_side(row, carry):
+        begin_block(row + 2, True)
+        return carry
+
+    lax.fori_loop(0, AR, begin_side, 0, unroll=6)
+    for row in (0, 1, AR + 2, AR + 3):
+        inside = tile > 0 if row < 2 else tile < TILES - 1
+        state = sx[row, :, 0:AC].astype(F32) + channel_weight * sst[row + 6 : row + 7, 128 : 128 + AC]
+        sx[row, :, 0:AC] = jnp.where(inside, state, 0.0).astype(BF)
+        begin_block(row, inside)
 
     def three(x, width):
         west_of = pltpu.roll(x, 1, 1)[:, 0:width]
@@ -318,14 +339,6 @@
 
     lax.fori_loop(0, OCN // 256, make_slots, 0)
 
-    def make_taps(step, carry):
-        base = pl.multiple_of(step * 256, 256)
-        for tap in range(TAPS):
-            inner = (taps_in[tap : tap + 1, pl.ds(base, 256)] - base) % 256
-            onetap[tap, :, pl.ds(base, 256)] = onehot(iota((256, 256), 0) == inner)
-        return carry
-
-    lax.fori_loop(0, OCN // 256, make_taps, 0)
     pltpu.make_async_copy(grecv.at[pl.ds(0, DEVICES - 1)], grecv.at[pl.ds(0, DEVICES - 1)], g_recv).wait()
 
     def turn(step, carry):
@@ -419,7 +432,8 @@
     layer(hwindow, 2, last_block)
     store.wait()
 
-    pltpu.make_async_copy(vsend.at[pl.ds(0, DEVICES - 1)], vsend.at[pl.ds(0, DEVICES - 1)], a_send).wait()
+    pltpu.make_async_copy(vsend.at[pl.ds(0, 7)], vsend.at[pl.ds(0, 7)], a_send).wait()
+    pltpu.make_async_copy(vturned.at[pl.ds(0, 15)], vturned.at[pl.ds(0, 15)], b_send).wait()
     pltpu.make_async_copy(gsend.at[pl.ds(0, DEVICES - 1)], gsend.at[pl.ds(0, DEVICES - 1)], g_send).wait()
 
 
@@ -460,8 +474,10 @@
             pltpu.VMEM((TAPS, OCN), I32),
             pltpu.VMEM((CH, AR, AC), BF),
             pltpu.VMEM((AR, CH, AC), BF),
-            pltpu.VMEM((DEVICES, 1, 128), F32),
-            pltpu.VMEM((DEVICES, 1, 128), F32),
+            pltpu.VMEM((8, 16, 256), F32),
+            pltpu.VMEM((8, 16, 256), F32),
+            pltpu.VMEM((16, 8, 256), F32),
+            pltpu.VMEM((16, 8, 256), F32),
             pltpu.VMEM((2, CH, 128), BF),
             pltpu.VMEM((6, CH, 128), BF),
             pltpu.VMEM((40, 768), F32),
@@ -470,7 +486,6 @@
             pltpu.VMEM((2, CH, RING), F32),
             pltpu.VMEM((2, 3 * CH, 3 * CH), BF),
             pltpu.VMEM((2 * CAP, SLOTS), BF),
-            pltpu.VMEM((2, CAP, 128), F32),
             pltpu.VMEM((AC, SLOTS), BF),
             pltpu.VMEM((DEVICES, 16, 128), BF),
             pltpu.VMEM((DEVICES, 16, 128), BF),
@@ -480,7 +495,7 @@
             pltpu.VMEM((2, CH, TAPS * CH), BF),
             pltpu.VMEM((CH, EXT), BF),
             pltpu.VMEM((CH, EXT), BF),
-            dma((6,)), dma, dma, dma((8,)), dma((8,)), dma((8,)), dma((8,)), dma, dma, dma((4,)), dma((4,)),
+            dma((6,)), dma, dma, dma, dma, dma((8,)), dma((8,)), dma((8,)), dma((8,)), dma, dma, dma((4,)), dma((4,)),
         ],
         compiler_params=pltpu.CompilerParams(
             collective_id=0, has_side_effects=True, vmem_limit_bytes=56 << 20

time: 67.3 us -> 63 us (0.936)
  Pallas kernels: 66.3 us -> 62 us
    pallas_call x1, Pallas kernels: 64 us -> 59.7 us  [shards(): pl.pallas_call(kernel, out_shape=(jax.ShapeDtypeStruct((CH, AR, AC), BF),...]
where the time goes in v2:
time: 63 us; the launch traced here: 62.8 us
  Pallas kernels  62 us (98%)
  between operations  0.8 us (1%)
    pallas_call x1, Pallas kernels, shards(): pl.pallas_call(kernel, out_shape=(jax.ShapeDtypeStruct((CH, AR, AC), BF),...  59.7 us
    pallas_call x1, Pallas kernels, shards(): pl.pallas_call(hand_over, out_shape=(jax.ShapeDtypeStruct((CH, AR, AC), B...  2.3 us

profile of v2, /device:TPU:0, one launch (start us, length us, event | category | flops | bytes accessed | tf_op | source)
XLA Modules:
  0.0 62.8 jit_solution(11608773848619264634)
XLA Ops:
  0.6 59.7 %level.1 = (bf16[64,24,512]{2,1,0:T(8,128)(2,1)}, bf16[64,2048]{1,0:T(8,128)(2,1)}) custom-call(bf16[64,24,512]{2,1,0:T(8,128)(2,1)} %air.1, bf16[64,2048]{1,0:T(8,128)(2,1)} %ocean.1, f32[1,64]{1,0:T(1,128)} %bitcast.3, bf16[3,3,64,64]{3,2,1,0:T(8,128)(2,1)} %w1.1, bf16[3,3,64,64]{3,2,1,0:T(8,128)(2,1)} %w2.1, bf16[9,64,64]{2,1,0:T(8,128)(2,1)} %m1.1, ...), custom_call_target="tpu_custom_call" | custom-call | tf_op jit(solution)/shard_map/level/pallas_call | solution.py:460
  60.4 2.3 %hand_over.1 = (bf16[64,24,512]{2,1,0:T(8,128)(2,1)}, bf16[64,2048]{1,0:T(8,128)(2,1)}) custom-call(bf16[64,24,512]{2,1,0:T(8,128)(2,1)} %get-tuple-element.4.air, bf16[64,2048]{1,0:T(8,128)(2,1)} %get-tuple-element.5.ocean), custom_call_target="tpu_custom_call" | custom-call | tf_op jit(solution)/shard_map/hand_over/pallas_call | solution.py:505

commit v3 on v2

--- a/solution.py
+++ b/solution.py
@@ -48,9 +48,9 @@
     air, ocean, heat, w1, w2, m1, m2, slot, cells, taps,
     air_out, ocean_out,
     air_in, w1_in, w2_in, m1_in, m2_in, taps_in, air_done, after,
-    vsend, vfirst, vturned, vrecv, cols, rcols, sst, sx, hx, acc, weights, picked_cols, onecol,
-    gsend, grecv, arrived, oneslot, onetap, mweights, window, hwindow,
-    local, a_send, a_recv, b_send, b_recv, r_send, r_recv, s_send, s_recv, g_send, g_recv, o_send, o_recv,
+    vsend, vrecv, cols, rcols, sst, sx, hx, acc, weights, picked_cols, onecol,
+    gsend, grecv, arrived, oneslot, mweights, window, hwindow,
+    local, entered, a_send, a_recv, r_send, r_recv, s_send, s_recv, g_send, g_recv, o_send, o_recv,
 ):
     face = lax.axis_index("face")
     tile = lax.axis_index("tile")
@@ -74,10 +74,9 @@
         return (face, lax.div(tile, 16) * 16 + number)
 
     barrier = pltpu.get_barrier_semaphore()
-    greeted = [outer_peer(lax.rem(outer + step, 8)) for step in range(1, 8)]
-    greeted += [inner_peer(lax.rem(inner_place + step, 16)) for step in range(1, 16)]
-    greeted += list(around)
-    for other in greeted:
+    near = [inner_peer(lax.rem(inner_place + step, 16)) for step in range(1, 16)]
+    far = [outer_peer(lax.rem(outer + step, 8)) for step in range(1, 8)]
+    for other in near + far:
         pl.semaphore_signal(barrier, inc=1, device_id=other, device_id_type=MESH)
 
     loads = [
@@ -91,19 +90,25 @@
 
     slots = slot[...]
     heat_row = ocean[0:16, :].astype(F32)[0:1]
-    source = onehot(iota((DEVICES, OCN), 0) == slots // CAP)
     here = iota((128, OCN), 0) == slots % CAP + CAP * lax.rem(me, 4)
     values = jnp.concatenate([jnp.where(here, heat_row, 0.0).astype(BF), onehot(here)], axis=0)
-    vsend[...] = dot_nt(source, values).reshape(8, 16, 256)
-
-    pl.semaphore_wait(barrier, len(greeted))
-    for step in range(1, 8):
-        other = lax.rem(outer + step, 8)
+    pl.semaphore_wait(barrier, len(near) + len(far))
+    for other in near:
+        pl.semaphore_signal(entered, inc=1, device_id=other, device_id_type=MESH)
+    source = onehot(iota((DEVICES, OCN), 0) == slots // CAP)
+    vsend[:, 0, :] = dot_nt(source, values)
+    pl.semaphore_wait(entered, len(near))
+
+    def send_values(step, carry):
+        other = lax.rem(me + step, DEVICES)
         pltpu.make_async_remote_copy(
-            src_ref=vsend.at[other], dst_ref=vfirst.at[outer], send_sem=a_send, recv_sem=a_recv,
-            device_id=outer_peer(other), device_id_type=MESH,
+            src_ref=vsend.at[other], dst_ref=vrecv.at[me], send_sem=a_send, recv_sem=a_recv,
+            device_id=where_of(other), device_id_type=MESH,
         ).start()
-    vfirst[outer] = vsend[outer]
+        return carry
+
+    lax.fori_loop(1, DEVICES, send_values, 0)
+    vrecv[me] = vsend[me]
 
     for copy in loads:
         copy.wait()
@@ -142,16 +147,6 @@
     ]
     for copy in air_rims:
         copy.start()
-
-    pltpu.make_async_copy(vfirst.at[pl.ds(0, 7)], vfirst.at[pl.ds(0, 7)], a_recv).wait()
-    vturned[...] = pltpu.einshape("bal->abl", vfirst[...])
-    for step in range(1, 16):
-        other = lax.rem(inner_place + step, 16)
-        pltpu.make_async_remote_copy(
-            src_ref=vturned.at[other], dst_ref=vrecv.at[inner_place], send_sem=b_send, recv_sem=b_recv,
-            device_id=inner_peer(other), device_id_type=MESH,
-        ).start()
-    vrecv[inner_place] = vturned[inner_place]
 
     def make_columns(step, carry):
         base = pl.multiple_of(step * 256, 256)
@@ -173,17 +168,15 @@
         jnp.where(iota((CH, CH), 0) == iota((CH, CH), 1), heat[...], 0.0), axis=1, keepdims=True
     )
 
-    pltpu.make_async_copy(vrecv.at[pl.ds(0, 15)], vrecv.at[pl.ds(0, 15)], b_recv).wait()
-    for quarter in range(4):
-        four = vrecv[quarter * 4 : quarter * 4 + 4]
-        lines = (four[0] + four[1]) + (four[2] + four[3])
-        for part in range(8):
-            base = (part * 4 + quarter) * 128
-            hit = iota((CAP, 128), 0) == cells[0:1, base : base + 128] // AC
-            for kind in range(2):
-                picked_cols[CAP * kind : CAP * (kind + 1), base : base + 128] = jnp.where(
-                    hit, lines[part : part + 1, kind * 128 : (kind + 1) * 128], 0.0
-                ).astype(BF)
+    pltpu.make_async_copy(vrecv.at[pl.ds(0, DEVICES - 1)], vrecv.at[pl.ds(0, DEVICES - 1)], a_recv).wait()
+    for block in range(SLOTS // 128):
+        base = block * 128
+        line = (vrecv[4 * block] + vrecv[4 * block + 1]) + (vrecv[4 * block + 2] + vrecv[4 * block + 3])
+        hit = iota((CAP, 128), 0) == cells[0:1, base : base + 128] // AC
+        for kind in range(2):
+            picked_cols[CAP * kind : CAP * (kind + 1), base : base + 128] = jnp.where(
+                hit, line[:, kind * 128 : (kind + 1) * 128], 0.0
+            ).astype(BF)
     sums = dot_nt(picked_cols[...], onecol[...])
     sst[8 : 8 + AR, 128 : 128 + AC] = sums[0:AR] / jnp.maximum(sums[CAP : CAP + AR], 1.0)
 
@@ -224,15 +217,6 @@
         sx[row, :, AC:RING] = ring_block(jnp.int32(AR - 2 + row), rcols[2].astype(F32), rcols[3].astype(F32))
         sx[AR + 2 + row, :, AC:RING] = ring_block(jnp.int32(row), rcols[4].astype(F32), rcols[5].astype(F32))
 
-    def make_taps(step, carry):
-        base = pl.multiple_of(step * 256, 256)
-        for tap in range(TAPS):
-            inner = (taps_in[tap : tap + 1, pl.ds(base, 256)] - base) % 256
-            onetap[tap, :, pl.ds(base, 256)] = onehot(iota((256, 256), 0) == inner)
-        return carry
-
-    lax.fori_loop(0, OCN // 256, make_taps, 0)
-
     for copy in sst_rims:
         copy.wait()
 
@@ -271,7 +255,7 @@
         hx[jnp.maximum(middle, 0)] = hidden.astype(BF)
         return carry
 
-    lax.fori_loop(0, AR + 4, first_conv, 0, unroll=AR + 4)
+    lax.fori_loop(0, AR + 4, first_conv, 0, unroll=7)
 
     def second_conv(row, carry):
         part = dot(weights[1], three(hx[row], AC))
@@ -282,7 +266,7 @@
         after[middle] = (sx[middle + 2, :, 0:AC].astype(F32) + total).astype(BF)
         return carry
 
-    lax.fori_loop(0, AR + 2, second_conv, 0, unroll=AR + 2)
+    lax.fori_loop(0, AR + 2, second_conv, 0, unroll=13)
 
     first_block = lax.div(me, 8)
 
@@ -381,8 +365,9 @@
         )
         groups = []
         for tap in range(TAPS):
-            part_of = (taps_in[tap : tap + 1, pl.ds(base, 256)] - base) // 256
-            found = dot(segments, onetap[tap, :, pl.ds(base, 256)])
+            index = taps_in[tap : tap + 1, pl.ds(base, 256)] - base
+            part_of = index // 256
+            found = dot(segments, onehot(iota((256, 256), 0) == index % 256))
             chosen = jnp.where(
                 part_of == 0, found[0:CH], jnp.where(part_of == 1, found[CH : 2 * CH], found[2 * CH : 3 * CH])
             )
@@ -417,7 +402,7 @@
             do_block(block)
             return carry
 
-        lax.fori_loop(1, 7, middle, 0, unroll=6)
+        lax.fori_loop(1, 7, middle, 0, unroll=2)
         for copy in copies:
             copy.wait()
         close_ends(buffer)
@@ -432,8 +417,7 @@
     layer(hwindow, 2, last_block)
     store.wait()
 
-    pltpu.make_async_copy(vsend.at[pl.ds(0, 7)], vsend.at[pl.ds(0, 7)], a_send).wait()
-    pltpu.make_async_copy(vturned.at[pl.ds(0, 15)], vturned.at[pl.ds(0, 15)], b_send).wait()
+    pltpu.make_async_copy(vsend.at[pl.ds(0, DEVICES - 1)], vsend.at[pl.ds(0, DEVICES - 1)], a_send).wait()
     pltpu.make_async_copy(gsend.at[pl.ds(0, DEVICES - 1)], gsend.at[pl.ds(0, DEVICES - 1)], g_send).wait()
 
 
@@ -474,10 +458,8 @@
             pltpu.VMEM((TAPS, OCN), I32),
             pltpu.VMEM((CH, AR, AC), BF),
             pltpu.VMEM((AR, CH, AC), BF),
-            pltpu.VMEM((8, 16, 256), F32),
-            pltpu.VMEM((8, 16, 256), F32),
-            pltpu.VMEM((16, 8, 256), F32),
-            pltpu.VMEM((16, 8, 256), F32),
+            pltpu.VMEM((DEVICES, 1, 256), F32),
+            pltpu.VMEM((DEVICES, 1, 256), F32),
             pltpu.VMEM((2, CH, 128), BF),
             pltpu.VMEM((6, CH, 128), BF),
             pltpu.VMEM((40, 768), F32),
@@ -491,11 +473,10 @@
             pltpu.VMEM((DEVICES, 16, 128), BF),
             pltpu.VMEM((128, OCN), BF),
             pltpu.VMEM((OCN, OCN), BF),
-            pltpu.VMEM((TAPS, 256, OCN), BF),
             pltpu.VMEM((2, CH, TAPS * CH), BF),
             pltpu.VMEM((CH, EXT), BF),
             pltpu.VMEM((CH, EXT), BF),
-            dma((6,)), dma, dma, dma, dma, dma((8,)), dma((8,)), dma((8,)), dma((8,)), dma, dma, dma((4,)), dma((4,)),
+            dma((6,)), pltpu.SemaphoreType.REGULAR, dma, dma, dma((8,)), dma((8,)), dma((8,)), dma((8,)), dma, dma, dma((4,)), dma((4,)),
         ],
         compiler_params=pltpu.CompilerParams(
             collective_id=0, has_side_effects=True, vmem_limit_bytes=56 << 20

time: 63 us -> 61.1 us (0.970)
  Pallas kernels: 62 us -> 60.3 us
    pallas_call x1, Pallas kernels: 59.7 us -> 58 us  [shards(): pl.pallas_call(kernel, out_shape=(jax.ShapeDtypeStruct((CH, AR, AC), BF),...]
where the time goes in v3:
time: 61.1 us; the launch traced here: 61 us
  Pallas kernels  60.3 us (99%)
  between operations  0.64 us (1%)
    pallas_call x1, Pallas kernels, shards(): pl.pallas_call(kernel, out_shape=(jax.ShapeDtypeStruct((CH, AR, AC), BF),...  58 us
    pallas_call x1, Pallas kernels, shards(): pl.pallas_call(hand_over, out_shape=(jax.ShapeDtypeStruct((CH, AR, AC), B...  2.3 us

profile of v3, /device:TPU:0, one launch (start us, length us, event | category | flops | bytes accessed | tf_op | source)
XLA Modules:
  0.0 61.0 jit_solution(16836881514259046283)
XLA Ops:
  0.6 58.0 %level.1 = (bf16[64,24,512]{2,1,0:T(8,128)(2,1)}, bf16[64,2048]{1,0:T(8,128)(2,1)}) custom-call(bf16[64,24,512]{2,1,0:T(8,128)(2,1)} %air.1, bf16[64,2048]{1,0:T(8,128)(2,1)} %ocean.1, f32[1,64]{1,0:T(1,128)} %bitcast.3, bf16[3,3,64,64]{3,2,1,0:T(8,128)(2,1)} %w1.1, bf16[3,3,64,64]{3,2,1,0:T(8,128)(2,1)} %w2.1, bf16[9,64,64]{2,1,0:T(8,128)(2,1)} %m1.1, ...), custom_call_target="tpu_custom_call" | custom-call | tf_op jit(solution)/shard_map/level/pallas_call | solution.py:444
  58.7 2.3 %hand_over.1 = (bf16[64,24,512]{2,1,0:T(8,128)(2,1)}, bf16[64,2048]{1,0:T(8,128)(2,1)}) custom-call(bf16[64,24,512]{2,1,0:T(8,128)(2,1)} %get-tuple-element.4.air, bf16[64,2048]{1,0:T(8,128)(2,1)} %get-tuple-element.5.ocean), custom_call_target="tpu_custom_call" | custom-call | tf_op jit(solution)/shard_map/hand_over/pallas_call | solution.py:486

commit v4 on v3

--- a/solution.py
+++ b/solution.py
@@ -45,19 +45,18 @@
 
 
 def kernel(
-    air, ocean, heat, w1, w2, m1, m2, slot, cells, taps,
+    air, ocean_hbm, heat_hbm, w1, w2, m1, m2, slot_hbm, cells_hbm, taps,
     air_out, ocean_out,
+    ocean, heat, slot, cells, ocean_done,
     air_in, w1_in, w2_in, m1_in, m2_in, taps_in, air_done, after,
     vsend, vrecv, cols, rcols, sst, sx, hx, acc, weights, picked_cols, onecol,
-    gsend, grecv, arrived, oneslot, mweights, window, hwindow,
-    local, entered, a_send, a_recv, r_send, r_recv, s_send, s_recv, g_send, g_recv, o_send, o_recv,
+    gsend, grecv, arrived, landed, oneslot, mweights, window, hwindow,
+    local, a_send, a_recv, r_send, r_recv, s_send, s_recv, g_send, g_recv, o_send, o_recv,
 ):
     face = lax.axis_index("face")
     tile = lax.axis_index("tile")
     me = face * TILES + tile
 
-    outer = face * 2 + lax.div(tile, 16)
-    inner_place = lax.rem(tile, 16)
     up = lax.rem(tile + TILES - 1, TILES)
     down = lax.rem(tile + 1, TILES)
     west = lax.rem(face + FACES - 1, FACES)
@@ -67,37 +66,39 @@
         (west, up), (west, down), (east, up), (east, down),
     )
 
-    def outer_peer(number):
-        return (lax.div(number, 2), lax.rem(number, 2) * 16 + inner_place)
-
-    def inner_peer(number):
-        return (face, lax.div(tile, 16) * 16 + number)
-
-    barrier = pltpu.get_barrier_semaphore()
-    near = [inner_peer(lax.rem(inner_place + step, 16)) for step in range(1, 16)]
-    far = [outer_peer(lax.rem(outer + step, 8)) for step in range(1, 8)]
-    for other in near + far:
-        pl.semaphore_signal(barrier, inc=1, device_id=other, device_id_type=MESH)
-
     loads = [
         pltpu.make_async_copy(src, dst, local.at[number])
         for number, (src, dst) in enumerate(
-            ((air, air_in), (w1, w1_in), (w2, w2_in), (m1, m1_in), (m2, m2_in), (taps, taps_in))
+            (
+                (slot_hbm, slot), (ocean_hbm, ocean), (cells_hbm, cells), (heat_hbm, heat), (air, air_in),
+                (w1, w1_in), (w2, w2_in), (m1, m1_in), (m2, m2_in), (taps, taps_in),
+            )
         )
     ]
     for copy in loads:
         copy.start()
 
+    barrier = pltpu.get_barrier_semaphore()
+
+    def greet(step, carry):
+        pl.semaphore_signal(
+            barrier, inc=1, device_id=where_of(lax.rem(me + step, DEVICES)), device_id_type=MESH
+        )
+        return carry
+
+    lax.fori_loop(0, 42, lambda step, carry: greet(3 * step + 3, greet(3 * step + 2, greet(3 * step + 1, carry))), 0)
+    greet(127, 0)
+
+    for copy in loads[:2]:
+        copy.wait()
+
     slots = slot[...]
     heat_row = ocean[0:16, :].astype(F32)[0:1]
     here = iota((128, OCN), 0) == slots % CAP + CAP * lax.rem(me, 4)
     values = jnp.concatenate([jnp.where(here, heat_row, 0.0).astype(BF), onehot(here)], axis=0)
-    pl.semaphore_wait(barrier, len(near) + len(far))
-    for other in near:
-        pl.semaphore_signal(entered, inc=1, device_id=other, device_id_type=MESH)
     source = onehot(iota((DEVICES, OCN), 0) == slots // CAP)
     vsend[:, 0, :] = dot_nt(source, values)
-    pl.semaphore_wait(entered, len(near))
+    pl.semaphore_wait(barrier, DEVICES - 1)
 
     def send_values(step, carry):
         other = lax.rem(me + step, DEVICES)
@@ -107,10 +108,11 @@
         ).start()
         return carry
 
-    lax.fori_loop(1, DEVICES, send_values, 0)
+    lax.fori_loop(0, 42, lambda step, carry: send_values(3 * step + 3, send_values(3 * step + 2, send_values(3 * step + 1, carry))), 0)
+    send_values(127, 0)
     vrecv[me] = vsend[me]
 
-    for copy in loads:
+    for copy in loads[2:]:
         copy.wait()
     sx[2 : AR + 2, :, 0:AC] = pltpu.einshape("crw->rcw", air_in[...])
 
@@ -164,6 +166,20 @@
     for number, weight in enumerate((m1_in, m2_in)):
         for tap in range(TAPS):
             mweights[number, :, tap * CH : (tap + 1) * CH] = weight[tap]
+    def make_slots(step, carry):
+        base = pl.multiple_of(step * 256, 256)
+        mark = slot[0:1, pl.ds(base, 256)]
+        row = mark // CAP * 16 + mark % 16
+
+        def fill(part, inner_carry):
+            first = pl.multiple_of(part * 256, 256)
+            oneslot[pl.ds(first, 256), pl.ds(base, 256)] = onehot(iota((256, 256), 0) + first == row)
+            return inner_carry
+
+        return lax.fori_loop(0, OCN // 256, fill, carry)
+
+    lax.fori_loop(0, OCN // 256, make_slots, 0)
+
     channel_weight = jnp.sum(
         jnp.where(iota((CH, CH), 0) == iota((CH, CH), 1), heat[...], 0.0), axis=1, keepdims=True
     )
@@ -285,63 +301,61 @@
                 state = jnp.where(row == part * 4 + inner, found[inner * CH : (inner + 1) * CH], state)
         return state
 
-    def ship(state, block, others):
+    def ship(state, block, others, number):
         flat = jnp.transpose(state).reshape(8, CAP, CH)
         pair = jnp.concatenate([flat[:, 0:16], flat[:, 16:32]], axis=2)
         gsend[pl.ds(pl.multiple_of(block * 8, 8), 8)] = pair.astype(BF)
         for inner in others:
             other = block * 8 + inner
             pltpu.make_async_remote_copy(
-                src_ref=gsend.at[other], dst_ref=grecv.at[me], send_sem=g_send, recv_sem=g_recv,
+                src_ref=gsend.at[other], dst_ref=grecv.at[me], send_sem=g_send, recv_sem=g_recv.at[number],
                 device_id=where_of(other), device_id_type=MESH,
             ).start()
 
     def coupling(step, state):
         found = find(block_of(step))
-        ship(state, block_of(step - 1), range(8))
+        ship(state, block_of(step - 1), range(8), lax.div(step - 2, 4))
         return found
 
     state = lax.fori_loop(2, DEVICES // 8 + 1, coupling, find(block_of(1)), unroll=3)
-    ship(state, first_block, [lax.rem(me + step, 8) for step in range(1, 8)])
+    ship(state, first_block, [lax.rem(me + step, 8) for step in range(1, 8)], 3)
     grecv[me] = gsend[me]
 
     air_done[...] = pltpu.einshape("rcw->crw", after[...])
     store = pltpu.make_async_copy(air_done, air_out, local.at[0])
     store.start()
 
-    def make_slots(step, carry):
-        base = pl.multiple_of(step * 256, 256)
-        mark = slot[0:1, pl.ds(base, 256)]
-        row = mark // CAP * 16 + mark % 16
-
-        def fill(part, inner_carry):
-            first = pl.multiple_of(part * 256, 256)
-            oneslot[pl.ds(first, 256), pl.ds(base, 256)] = onehot(iota((256, 256), 0) + first == row)
-            return inner_carry
-
-        return lax.fori_loop(0, OCN // 256, fill, carry)
-
-    lax.fori_loop(0, OCN // 256, make_slots, 0)
-
-    pltpu.make_async_copy(grecv.at[pl.ds(0, DEVICES - 1)], grecv.at[pl.ds(0, DEVICES - 1)], g_recv).wait()
-
-    def turn(step, carry):
-        eight = grecv[pl.ds(pl.multiple_of(step * 8, 8), 8)].reshape(128, 128)
-        arrived[:, pl.ds(pl.multiple_of(step * 128, 128), 128)] = jnp.transpose(eight.astype(F32)).astype(BF)
-        return carry
-
-    lax.fori_loop(0, DEVICES // 8, turn, 0, unroll=8)
-
-    def force(step, carry):
-        base = pl.multiple_of(step * 256, 256)
-        late = (slot[0:1, pl.ds(base, 256)] // 16) % 2 == 1
-        found = dot(arrived[...], oneslot[:, pl.ds(base, 256)])
-        forcing = jnp.where(late, found[CH : 2 * CH], found[0:CH])
-        begun = ocean[:, pl.ds(base, 256)].astype(F32) + forcing
-        window[:, pl.ds(base + HALO, 256)] = begun.astype(BF)
-        return carry
-
-    lax.fori_loop(0, OCN // 256, force, 0, unroll=4)
+    def quarter(number):
+        count = 32 if number < 3 else 31
+        pltpu.make_async_copy(grecv.at[pl.ds(0, count)], grecv.at[pl.ds(0, count)], g_recv.at[number]).wait()
+        sources = [
+            lax.rem(first_block + DEVICES // 8 - (4 * number + turn), DEVICES // 8) for turn in range(1, 5)
+        ]
+        for place, block in enumerate(sources):
+            eight = grecv[pl.ds(pl.multiple_of(block * 8, 8), 8)].reshape(128, 128)
+            arrived[:, place * 128 : (place + 1) * 128] = jnp.transpose(eight.astype(F32)).astype(BF)
+
+        def select(step, carry):
+            base = pl.multiple_of(step * 256, 256)
+            marks = jnp.concatenate(
+                [oneslot[pl.ds(pl.multiple_of(block * 128, 128), 128), pl.ds(base, 256)] for block in sources], axis=0
+            )
+            found = dot(arrived[...], marks)
+            if number > 0:
+                found = found + landed[:, pl.ds(base, 256)]
+            if number < 3:
+                landed[:, pl.ds(base, 256)] = found
+            else:
+                late = (slot[0:1, pl.ds(base, 256)] // 16) % 2 == 1
+                forcing = jnp.where(late, found[CH : 2 * CH], found[0:CH])
+                begun = ocean[:, pl.ds(base, 256)].astype(F32) + forcing
+                window[:, pl.ds(base + HALO, 256)] = begun.astype(BF)
+            return carry
+
+        lax.fori_loop(0, OCN // 256, select, 0, unroll=4)
+
+    for number in range(4):
+        quarter(number)
 
     previous = where_of(lax.rem(me + DEVICES - 1, DEVICES))
     following = where_of(lax.rem(me + 1, DEVICES))
@@ -382,7 +396,7 @@
     def last_block(block):
         total = mix(hwindow, 1, block)
         base = pl.multiple_of(block * 256, 256)
-        ocean_out[:, pl.ds(base, 256)] = (window[:, pl.ds(base + HALO, 256)].astype(F32) + total).astype(BF)
+        ocean_done[:, pl.ds(base, 256)] = (window[:, pl.ds(base + HALO, 256)].astype(F32) + total).astype(BF)
 
     def close_ends(buffer):
         @pl.when(me == 0)
@@ -393,7 +407,7 @@
         def _():
             buffer[:, EXT - HALO : EXT] = jnp.zeros((CH, HALO), BF)
 
-    def layer(buffer, first, do_block):
+    def layer(buffer, first, do_block, between):
         copies = ocean_rims(buffer, first)
         for copy in copies:
             copy.start()
@@ -403,6 +417,7 @@
             return carry
 
         lax.fori_loop(1, 7, middle, 0, unroll=2)
+        between()
         for copy in copies:
             copy.wait()
         close_ends(buffer)
@@ -413,8 +428,16 @@
 
         lax.fori_loop(0, 2, ends, 0, unroll=2)
 
-    layer(window, 0, hidden_block)
-    layer(hwindow, 2, last_block)
+    stores = [
+        pltpu.make_async_copy(ocean_done.at[:, first:last], ocean_out.at[:, first:last], local.at[number])
+        for number, first, last in ((1, 256, 1792), (2, 0, 256), (3, 1792, 2048))
+    ]
+    layer(window, 0, hidden_block, lambda: None)
+    layer(hwindow, 2, last_block, stores[0].start)
+    stores[1].start()
+    stores[2].start()
+    for copy in stores:
+        copy.wait()
     store.wait()
 
     pltpu.make_async_copy(vsend.at[pl.ds(0, DEVICES - 1)], vsend.at[pl.ds(0, DEVICES - 1)], a_send).wait()
@@ -438,7 +461,6 @@
 
 
 def shards(atmos, ocean, heat, w1, w2, m1, m2, slot, cells, taps):
-    vmem = pl.BlockSpec(memory_space=pltpu.VMEM)
     dma = pltpu.SemaphoreType.DMA
     anywhere = pl.BlockSpec(memory_space=pl.ANY)
     results = pl.pallas_call(
@@ -447,9 +469,14 @@
             jax.ShapeDtypeStruct((CH, AR, AC), BF),
             jax.ShapeDtypeStruct((CH, OCN), BF),
         ),
-        in_specs=[anywhere, vmem, vmem] + [anywhere] * 4 + [vmem, vmem, anywhere],
-        out_specs=(anywhere, vmem),
+        in_specs=[anywhere] * 10,
+        out_specs=(anywhere, anywhere),
         scratch_shapes=[
+            pltpu.VMEM((CH, OCN), BF),
+            pltpu.VMEM((1, CH), F32),
+            pltpu.VMEM((1, OCN), I32),
+            pltpu.VMEM((1, SLOTS), I32),
+            pltpu.VMEM((CH, OCN), BF),
             pltpu.VMEM((CH, AR, AC), BF),
             pltpu.VMEM((3, 3, CH, CH), BF),
             pltpu.VMEM((3, 3, CH, CH), BF),
@@ -471,12 +498,13 @@
             pltpu.VMEM((AC, SLOTS), BF),
             pltpu.VMEM((DEVICES, 16, 128), BF),
             pltpu.VMEM((DEVICES, 16, 128), BF),
-            pltpu.VMEM((128, OCN), BF),
+            pltpu.VMEM((128, 512), BF),
+            pltpu.VMEM((128, OCN), F32),
             pltpu.VMEM((OCN, OCN), BF),
             pltpu.VMEM((2, CH, TAPS * CH), BF),
             pltpu.VMEM((CH, EXT), BF),
             pltpu.VMEM((CH, EXT), BF),
-            dma((6,)), pltpu.SemaphoreType.REGULAR, dma, dma, dma((8,)), dma((8,)), dma((8,)), dma((8,)), dma, dma, dma((4,)), dma((4,)),
+            dma((10,)), dma, dma, dma((8,)), dma((8,)), dma((8,)), dma((8,)), dma, dma((4,)), dma((4,)), dma((4,)),
         ],
         compiler_params=pltpu.CompilerParams(
             collective_id=0, has_side_effects=True, vmem_limit_bytes=56 << 20

time: 61.1 us -> 57.7 us (0.944)
  Pallas kernels: 60.3 us -> 56.9 us
    pallas_call x1, Pallas kernels: 58 us -> 54.6 us  [shards(): pl.pallas_call(kernel, out_shape=(jax.ShapeDtypeStruct((CH, AR, AC), BF),...]
where the time goes in v4:
time: 57.7 us; the launch traced here: 57.6 us
  Pallas kernels  56.9 us (99%)
  between operations  0.64 us (1%)
    pallas_call x1, Pallas kernels, shards(): pl.pallas_call(kernel, out_shape=(jax.ShapeDtypeStruct((CH, AR, AC), BF),...  54.6 us
    pallas_call x1, Pallas kernels, shards(): pl.pallas_call(hand_over, out_shape=(jax.ShapeDtypeStruct((CH, AR, AC), B...  2.3 us

profile of v4, /device:TPU:0, one launch (start us, length us, event | category | flops | bytes accessed | tf_op | source)
XLA Modules:
  0.0 57.6 jit_solution(16668319816175947450)
XLA Ops:
  0.6 54.6 %level.1 = (bf16[64,24,512]{2,1,0:T(8,128)(2,1)}, bf16[64,2048]{1,0:T(8,128)(2,1)}) custom-call(bf16[64,24,512]{2,1,0:T(8,128)(2,1)} %air.1, bf16[64,2048]{1,0:T(8,128)(2,1)} %ocean_hbm.1, f32[1,64]{1,0:T(1,128)} %bitcast.3, bf16[3,3,64,64]{3,2,1,0:T(8,128)(2,1)} %w1.1, bf16[3,3,64,64]{3,2,1,0:T(8,128)(2,1)} %w2.1, bf16[9,64,64]{2,1,0:T(8,128)(2,1)} %m1.1, ...), custom_call_target="tpu_custom_call" | custom-call | tf_op jit(solution)/shard_map/level/pallas_call | solution.py:466
  55.3 2.3 %hand_over.1 = (bf16[64,24,512]{2,1,0:T(8,128)(2,1)}, bf16[64,2048]{1,0:T(8,128)(2,1)}) custom-call(bf16[64,24,512]{2,1,0:T(8,128)(2,1)} %get-tuple-element.4.air, bf16[64,2048]{1,0:T(8,128)(2,1)} %get-tuple-element.5.ocean), custom_call_target="tpu_custom_call" | custom-call | tf_op jit(solution)/shard_map/hand_over/pallas_call | solution.py:514

commit v5 on v4

--- a/solution.py
+++ b/solution.py
@@ -114,7 +114,21 @@
 
     for copy in loads[2:]:
         copy.wait()
-    sx[2 : AR + 2, :, 0:AC] = pltpu.einshape("crw->rcw", air_in[...])
+    def rim(number, src, dst, send, recv):
+        return pltpu.make_async_remote_copy(
+            src_ref=src, dst_ref=dst, send_sem=send.at[number], recv_sem=recv.at[number],
+            device_id=around[number], device_id_type=MESH,
+        )
+
+    for first in (0, 16):
+        sx[first + 2 : first + 10, :, 0:AC] = pltpu.einshape("crw->rcw", air_in[:, first : first + 8, :])
+    air_rims = [
+        rim(0, sx.at[2:4, :, 0:AC], sx.at[AR + 2 : AR + 4, :, 0:AC], r_send, r_recv),
+        rim(1, sx.at[AR : AR + 2, :, 0:AC], sx.at[0:2, :, 0:AC], r_send, r_recv),
+    ]
+    for copy in air_rims:
+        copy.start()
+    sx[10:18, :, 0:AC] = pltpu.einshape("crw->rcw", air_in[:, 8:16, :])
 
     lane = iota((CH, 128), 1)
 
@@ -131,15 +145,7 @@
     cols[0] = left.astype(BF)
     cols[1] = right.astype(BF)
 
-    def rim(number, src, dst, send, recv):
-        return pltpu.make_async_remote_copy(
-            src_ref=src, dst_ref=dst, send_sem=send.at[number], recv_sem=recv.at[number],
-            device_id=around[number], device_id_type=MESH,
-        )
-
-    air_rims = [
-        rim(0, sx.at[2:4, :, 0:AC], sx.at[AR + 2 : AR + 4, :, 0:AC], r_send, r_recv),
-        rim(1, sx.at[AR : AR + 2, :, 0:AC], sx.at[0:2, :, 0:AC], r_send, r_recv),
+    column_rims = [
         rim(2, cols.at[0], rcols.at[1], r_send, r_recv),
         rim(3, cols.at[1], rcols.at[0], r_send, r_recv),
         rim(4, cols.at[0], rcols.at[5], r_send, r_recv),
@@ -147,8 +153,9 @@
         rim(6, cols.at[1], rcols.at[4], r_send, r_recv),
         rim(7, cols.at[1], rcols.at[2], r_send, r_recv),
     ]
-    for copy in air_rims:
+    for copy in column_rims:
         copy.start()
+    air_rims += column_rims
 
     def make_columns(step, carry):
         base = pl.multiple_of(step * 256, 256)
@@ -317,7 +324,7 @@
         ship(state, block_of(step - 1), range(8), lax.div(step - 2, 4))
         return found
 
-    state = lax.fori_loop(2, DEVICES // 8 + 1, coupling, find(block_of(1)), unroll=3)
+    state = lax.fori_loop(2, DEVICES // 8 + 1, coupling, find(block_of(1)), unroll=5)
     ship(state, first_block, [lax.rem(me + step, 8) for step in range(1, 8)], 3)
     grecv[me] = gsend[me]
 
@@ -372,14 +379,38 @@
             ),
         ]
 
+    def lane_pick(wide, index):
+        halves = []
+        for half in range(2):
+            reach = jnp.broadcast_to(index[:, half * 128 : (half + 1) * 128] - 128 * half, (8, 128))
+            inner = reach % 128
+            part_of = reach // 128
+            groups = []
+            for group in range(CH // 8):
+                parts = []
+                for part in range(half, half + 5):
+                    row = (part // 2) * CH + group * 8
+                    column = (part % 2) * 128
+                    parts.append(wide[row : row + 8, column : column + 128])
+                found = jnp.take_along_axis(parts[0], inner, axis=1)
+                for part in range(1, 5):
+                    found = jnp.where(part_of == part, jnp.take_along_axis(parts[part], inner, axis=1), found)
+                groups.append(found)
+            halves.append(jnp.concatenate(groups, axis=0))
+        return jnp.concatenate(halves, axis=1)
+
     def mix(buffer, number, block):
         base = pl.multiple_of(block * 256, 256)
         segments = jnp.concatenate(
             [buffer[:, pl.ds(pl.multiple_of(base + 256 * part, 256), 256)] for part in range(3)], axis=0
         )
+        wide = segments.astype(F32)
         groups = []
         for tap in range(TAPS):
             index = taps_in[tap : tap + 1, pl.ds(base, 256)] - base
+            if tap % 3 == 2:
+                groups.append(lane_pick(wide, index).astype(BF))
+                continue
             part_of = index // 256
             found = dot(segments, onehot(iota((256, 256), 0) == index % 256))
             chosen = jnp.where(

time: 57.7 us -> 57.4 us (level)
  no operation moved by 1% of the time
where the time goes in v5:
time: 57.4 us; the launch traced here: 57.2 us
  Pallas kernels  56.6 us (99%)
  between operations  0.64 us (1%)
    pallas_call x1, Pallas kernels, shards(): pl.pallas_call(kernel, out_shape=(jax.ShapeDtypeStruct((CH, AR, AC), BF),...  54.3 us
    pallas_call x1, Pallas kernels, shards(): pl.pallas_call(hand_over, out_shape=(jax.ShapeDtypeStruct((CH, AR, AC), B...  2.3 us

profile of v5, /device:TPU:0, one launch (start us, length us, event | category | flops | bytes accessed | tf_op | source)
XLA Modules:
  0.0 57.2 jit_solution(18168705440124744112)
XLA Ops:
  0.6 54.3 %level.1 = (bf16[64,24,512]{2,1,0:T(8,128)(2,1)}, bf16[64,2048]{1,0:T(8,128)(2,1)}) custom-call(bf16[64,24,512]{2,1,0:T(8,128)(2,1)} %air.1, bf16[64,2048]{1,0:T(8,128)(2,1)} %ocean_hbm.1, f32[1,64]{1,0:T(1,128)} %bitcast.3, bf16[3,3,64,64]{3,2,1,0:T(8,128)(2,1)} %w1.1, bf16[3,3,64,64]{3,2,1,0:T(8,128)(2,1)} %w2.1, bf16[9,64,64]{2,1,0:T(8,128)(2,1)} %m1.1, ...), custom_call_target="tpu_custom_call" | custom-call | tf_op jit(solution)/shard_map/level/pallas_call | solution.py:497
  54.9 2.3 %hand_over.1 = (bf16[64,24,512]{2,1,0:T(8,128)(2,1)}, bf16[64,2048]{1,0:T(8,128)(2,1)}) custom-call(bf16[64,24,512]{2,1,0:T(8,128)(2,1)} %get-tuple-element.4.air, bf16[64,2048]{1,0:T(8,128)(2,1)} %get-tuple-element.5.ocean), custom_call_target="tpu_custom_call" | custom-call | tf_op jit(solution)/shard_map/hand_over/pallas_call | solution.py:545
